TPU v7x, 256 devices: a whole 4x4x8 slice. The times are simulated.
256 devices in a mesh: dp: 8 (over x, core), ctx: 32 (over y, z).
Axes of the slice: x: 4, y: 4, z: 8, core: 2. Of those that a mesh axis runs over, the one named last changes fastest.
Arguments:
- grad_out: bfloat16 [8, 10240, 2048], P('dp', 'ctx'), may hold values from -6 to 6
- chosen: int32 [8, 2560], P('dp', 'ctx'), may hold values from 0 to 319, as said below
- counts: int32 [8, 32], P('dp', 'ctx'), may hold values from 1 to 80, 1280 in all within a row
- queries: bfloat16 [8, 2560, 1024], P('dp', 'ctx'), may hold values from -136 to 136
- keys: bfloat16 [8, 2560, 1024], P('dp', 'ctx'), may hold values from -4 to 4
- values: bfloat16 [8, 2560, 1024], P('dp', 'ctx'), may hold values from -6 to 6
- router_logit: float32 [8, 2560], P('dp', 'ctx'), may hold values from -8 to 8
- out_weight: bfloat16 [1024, 2048], replicated, may hold values from -0.1875 to 0.1875
Outputs:
- d_queries: bfloat16 [8, 2560, 1024], P('dp', 'ctx')
- d_keys: bfloat16 [8, 2560, 1024], P('dp', 'ctx')
- d_values: bfloat16 [8, 2560, 1024], P('dp', 'ctx')
- d_logit: float32 [8, 2560], P('dp', 'ctx')
- d_weight: float32 [1024, 2048], P(None, 'ctx')
Inputs may be any that keep to these rules, and one draw needn't show every extreme that they name: Each ctx shard's 80 entries are distinct local positions in ascending order; the first counts of them are that shard's chosen tokens. The counts of one sequence sum to 1280.
All inputs are finite; a program needn't handle non-finite values. No bound on the sum of `counts` on one device may be relied on, other than what follows from the above.
Results may differ from a plain program's by a relative error of at most 0.03.
Values may be sent and summed in bfloat16 or wider, within the bound.
A program may use at most 192 MiB of HBM per device.

v0:
```python
import math

import jax
import jax.numpy as jnp
from jax import lax
from jax.sharding import PartitionSpec as P

HEAD_DIM = 128


NEG_FILL = -1e30


def on_device(grad_out, chosen, counts, queries, keys, values, router_logit, out_weight):
    cap_rows = queries.shape[1]
    width = queries.shape[2]
    heads = width // HEAD_DIM
    scale = 1.0 / math.sqrt(HEAD_DIM)
    my_shard = lax.axis_index("ctx")
    shards = lax.axis_size("ctx")
    total_slots = shards * cap_rows
    local_slot = jnp.arange(cap_rows, dtype=jnp.int32)
    my_slots = my_shard * cap_rows + local_slot
    live_mine = local_slot < counts[0, 0]
    picked = jnp.where(live_mine[:, None], grad_out[0][chosen[0]], jnp.zeros((), grad_out.dtype))
    all_keys, all_values, all_counts = (
        lax.all_gather(keys, "ctx", axis=1, tiled=True),
        lax.all_gather(values, "ctx", axis=1, tiled=True),
        lax.all_gather(counts, "ctx", axis=1, tiled=True),
    )
    every_slot = jnp.arange(total_slots, dtype=jnp.int32)
    live_every = every_slot % cap_rows < jnp.repeat(
        all_counts[0], cap_rows, total_repeat_length=total_slots
    )
    query_heads = queries[0].reshape(cap_rows, heads, HEAD_DIM)
    key_heads = all_keys[0].reshape(total_slots, heads, HEAD_DIM)
    value_heads = all_values[0].reshape(total_slots, heads, HEAD_DIM)
    allowed = live_mine[:, None] & live_every[None, :] & (
        every_slot[None, :] <= my_slots[:, None]
    ) | (every_slot[None, :] == my_slots[:, None])
    scores = (
        jnp.einsum("qhd,khd->hqk", query_heads, key_heads, preferred_element_type=jnp.float32)
        * scale
    )
    scores = jnp.where(allowed[None], scores, NEG_FILL)
    row_max = jnp.max(scores, axis=2, keepdims=True)
    expo = jnp.where(allowed[None], jnp.exp(scores - row_max), 0.0)
    row_total = jnp.sum(expo, axis=2, keepdims=True)
    probs = expo / row_total
    probs_b = probs.astype(jnp.bfloat16)
    attended = (
        jnp.einsum("hqk,khd->qhd", probs_b, value_heads, preferred_element_type=jnp.float32)
        .reshape(cap_rows, width)
        .astype(jnp.bfloat16)
    )
    projected = jnp.dot(attended, out_weight, preferred_element_type=jnp.float32)
    gate = jax.nn.sigmoid(router_logit[0])
    d_logit = jnp.where(
        live_mine,
        gate * (1.0 - gate) * jnp.sum(picked.astype(jnp.float32) * projected, axis=1),
        0.0,
    )
    d_block = (gate[:, None] * picked.astype(jnp.float32)).astype(jnp.bfloat16)
    d_attended = jnp.einsum(
        "qb,ab->qa", d_block, out_weight, preferred_element_type=jnp.float32
    ).astype(jnp.bfloat16)
    d_att_heads = d_attended.reshape(cap_rows, heads, HEAD_DIM)
    delta = jnp.sum(
        d_att_heads.astype(jnp.float32)
        * attended.reshape(cap_rows, heads, HEAD_DIM).astype(jnp.float32),
        axis=2,
    )
    d_probs = jnp.einsum(
        "qhd,khd->hqk", d_att_heads, value_heads, preferred_element_type=jnp.float32
    )
    d_scores = (probs * (d_probs - delta.T[:, :, None]) * scale).astype(jnp.bfloat16)
    d_queries = (
        jnp.einsum("hqk,khd->qhd", d_scores, key_heads, preferred_element_type=jnp.float32)
        .reshape(cap_rows, width)
        .astype(jnp.bfloat16)
    )
    count = cap_rows * lax.axis_size("ctx")
    score_part = lax.slice_in_dim(d_scores, 0, count, axis=2)
    prob_part = lax.slice_in_dim(probs_b, 0, count, axis=2)
    key_grad = jnp.einsum(
        "hqk,qhd->khd", score_part, query_heads, preferred_element_type=jnp.float32
    ).reshape(count, width)
    value_grad = jnp.einsum(
        "hqk,qhd->khd", prob_part, d_att_heads, preferred_element_type=jnp.float32
    ).reshape(count, width)
    summed = lax.psum_scatter(
        jnp.concatenate([key_grad, value_grad], axis=1).astype(jnp.bfloat16),
        "ctx",
        scatter_dimension=0,
        tiled=True,
    ).astype(jnp.float32)
    d_keys = summed[:, :width].astype(jnp.bfloat16)
    d_values = summed[:, width:].astype(jnp.bfloat16)
    weight_part = jnp.einsum("qa,qb->ab", attended, d_block, preferred_element_type=jnp.float32)
    column_sum = lax.psum_scatter(
        weight_part.astype(jnp.bfloat16), "ctx", scatter_dimension=1, tiled=True
    )
    d_weight = lax.psum(column_sum, "dp").astype(jnp.float32)
    return (d_queries[None], d_keys[None], d_values[None], d_logit[None], d_weight)


def solution(mesh):
    return jax.shard_map(
        on_device,
        mesh=mesh,
        in_specs=(
            P("dp", "ctx", None),
            P("dp", "ctx"),
            P("dp", "ctx"),
            P("dp", "ctx", None),
            P("dp", "ctx", None),
            P("dp", "ctx", None),
            P("dp", "ctx"),
            P(),
        ),
        out_specs=(
            P("dp", "ctx", None),
            P("dp", "ctx", None),
            P("dp", "ctx", None),
            P("dp", "ctx"),
            P(None, "ctx"),
        ),
        check_vma=False,
    )
```

profile of v0, /device:TPU:1, one launch (start us, length us, event | category | flops | bytes accessed | tf_op | source)
XLA Modules:
  0.0 728.6 jit_solution(1713880640219971878)
XLA Ops:
  7.2 0.7 all-gather.3.cloned.1.call-update
  8.0 0.7 all-gather.5.cloned.1.call-update
  9.4 0.9 copy.56
  10.3 1.3 dynamic-slice.6
  12.2 0.8 gather_fusion
  13.7 20.4 %all-reduce = s32[32]{0:T(128)S(1)} all-reduce(s32[32]{0:T(128)S(1)} %bitcast_dynamic-update-slice_fusion), channel_id=1, replica_groups=mesh['dp'=8,'ctx'=32] {'ctx'}, use_global_device_ids=true, to_apply=%add | all-reduce | flops 32 | bytes 256
  34.1 0.7 fusion.42
  34.9 0.7 fusion.41
  35.6 20.9 %fusion.29 = pred[2560]{0:T(1024)(128)(4,1)S(1)} fusion(pred[2560]{0:T(1024)(128)(4,1)} %constant.171, pred[2560]{0:T(1024)(128)(4,1)} %constant.172, pred[2560]{0:T(1024)(128)(4,1)} %constant.173, pred[2560]{0:T(1024)(128)(4,1)} %constant.174, pred[2560]{0:T(1024)(128)(4,1)} %constant.175, pred[2560]{0:T(1024)(128)(4,1)} %constant.176, ...), kind=kLoop, calls=%fused_computation.46 | loop fusion | flops 97280 | bytes 82048 | tf_op jit(solution)/shard_map/lt | solution.py:32
  56.8 40.4 %all-gather.3.cloned.1.call-done = bf16[1,2560,1024]{2,1,0:T(8,128)(2,1)} async-done(((bf16[1,80,1024]{2,1,0:T(8,128)(2,1)}), bf16[1,2560,1024]{2,1,0:T(8,128)(2,1)}) %all-gather.3.cloned.1.call-update) | async-done | bytes 5242896 | tf_op jit(solution)/shard_map/all_gather | solution.py:27
  97.2 7.9 %copy.35 = bf16[1,2560,1024]{1,2,0:T(8,128)(2,1)} copy(bf16[1,2560,1024]{2,1,0:T(8,128)(2,1)} %all-gather.3.cloned.1.call-done) | data formatting | bytes 10485760 | tf_op jit(solution)/shard_map/all_gather | solution.py:27
  105.2 8.2 %fusion.43 = (f32[8,80]{1,0:T(8,128)S(1)}, f32[8,80,2560]{2,1,0:T(8,128)}) fusion(pred[80,2560]{1,0:T(8,128)(4,1)S(1)} %fusion.10, bf16[2560,8,128]{0,2,1:T(8,128)(2,1)} %bitcast.96, bf16[80,8,128]{2,1,0:T(8,128)(2,1)S(1)} %bitcast.102), kind=kOutput, calls=%fused_computation.65 | convolution fusion | flops 427624960 | bytes 12167680 | tf_op jit(solution)/shard_map/sub | solution.py:47
  113.4 68.7 %all-gather.5.cloned.1.call-done = bf16[1,2560,1024]{2,1,0:T(8,128)(2,1)} async-done(((bf16[1,80,1024]{2,1,0:T(8,128)(2,1)}), bf16[1,2560,1024]{2,1,0:T(8,128)(2,1)}) %all-gather.5.cloned.1.call-update) | async-done | bytes 5242896 | tf_op jit(solution)/shard_map/all_gather | solution.py:28
  182.1 7.9 %copy.38 = bf16[1,2560,1024]{1,2,0:T(8,128)(2,1)} copy(bf16[1,2560,1024]{2,1,0:T(8,128)(2,1)} %all-gather.5.cloned.1.call-done) | data formatting | bytes 10485760 | tf_op jit(solution)/shard_map/all_gather | solution.py:28
  190.0 6.5 convolution_convert_fusion.4
  196.5 1.0 fusion.6
  198.0 3.4 convolution_convert_fusion.2
  201.6 3.6 fusion.7
  205.2 6.8 convolution_convert_fusion
  212.1 8.0 %copy.48 = bf16[2560,1024]{1,0:T(8,128)(2,1)} copy(bf16[2560,1024]{0,1:T(8,128)(2,1)} %bitcast.101) | data formatting | bytes 10485760 | tf_op jit(solution)/shard_map/reshape | solution.py:90
  220.3 5.4 multiply_convert_fusion
  225.6 1.7 copy-done.3
  227.3 3.9 convolution_convert_fusion.1
  231.2 8.0 %copy.47 = bf16[2560,1024]{1,0:T(8,128)(2,1)} copy(bf16[2560,1024]{0,1:T(8,128)(2,1)} %bitcast.98) | data formatting | bytes 10485760 | tf_op jit(solution)/shard_map/reshape | solution.py:87
  239.2 177.9 %reduce-scatter.5.cloned.1.call-done = bf16[1024,64]{0,1:T(8,128)(2,1)} async-done(((bf16[1024,2048]{0,1:T(8,128)(2,1)}), bf16[1024,64]{0,1:T(8,128)(2,1)}) %reduce-scatter.5.cloned.1.call-update) | async-done | bytes 131088 | tf_op jit(solution)/shard_map/reduce_scatter | solution.py:100
  417.2 9.8 %pad_maximum_fusion = bf16[2560,2048]{1,0:T(8,128)(2,1)} fusion(bf16[2560,1024]{1,0:T(8,128)(2,1)} %copy.48, bf16[2560,1024]{1,0:T(8,128)(2,1)} %copy.47), kind=kLoop, calls=%fused_computation.2 | loop fusion | flops 20971520 | bytes 20971520 | tf_op jit(solution)/shard_map/concatenate | solution.py:92
  427.1 5.5 fusion.8
  432.6 0.7 convert_element_type.71
  433.3 51.6 %all-reduce.3.cloned.1.call-done = bf16[1024,64]{0,1:T(8,128)(2,1)} async-done(((bf16[1024,64]{0,1:T(8,128)(2,1)}), bf16[1024,64]{0,1:T(8,128)(2,1)}) %all-reduce.3.cloned.1.call-update) | async-done | bytes 131088 | tf_op jit(solution)/shard_map/psum | solution.py:103
  484.9 1.6 convert_element_type.74
  486.6 233.7 %reduce-scatter.3.cloned.1.call-done = bf16[80,2048]{1,0:T(8,128)(2,1)} async-done(((bf16[2560,2048]{1,0:T(8,128)(2,1)}), bf16[80,2048]{1,0:T(8,128)(2,1)}) %reduce-scatter.3.cloned.1.call-update) | async-done | bytes 327696 | tf_op jit(solution)/shard_map/reduce_scatter | solution.py:91
  720.3 1.7 slice_bitcast_fusion
  (27 shorter events, 2.9 us)
Async XLA Ops:
  7.2 5.1 copy-start
  7.2 90.1 %all-gather.3.cloned.1.call-start = ((), (), s32[]{:S(2)}) async-start(), calls=%async_computation.2 | async-start | bytes 5406720 | tf_op jit(solution)/shard_map/all_gather | solution.py:27
  7.9 174.2 %all-gather.5.cloned.1.call-start = ((), (), s32[]{:S(2)}) async-start(), calls=%async_computation.3 | async-start | bytes 5406720 | tf_op jit(solution)/shard_map/all_gather | solution.py:28
  8.7 408.4 %reduce-scatter.5.cloned.1.call-start = ((), (), s32[]{:S(2)}) async-start(), calls=%async_computation.5 | async-start | bytes 4325376 | tf_op jit(solution)/shard_map/reduce_scatter | solution.py:100
  190.0 6.5 copy-start.2
  190.0 7.5 %copy-start.4 = (f32[1,80]{1,0:T(1,128)S(1)}, f32[1,80]{1,0:T(1,128)}, u32[]{:S(2)}) copy-start(f32[1,80]{1,0:T(1,128)} %param.16) | copy-start | bytes 964
  201.4 283.5 %all-reduce.3.cloned.1.call-start = ((), (), s32[]{:S(2)}) async-start(), calls=%async_computation.6 | async-start | bytes 262144 | tf_op jit(solution)/shard_map/psum | solution.py:103
  225.6 1.7 copy-start.3
  417.1 303.2 %reduce-scatter.3.cloned.1.call-start = ((), (), s32[]{:S(2)}) async-start(), calls=%async_computation.4 | async-start | bytes 10813440 | tf_op jit(solution)/shard_map/reduce_scatter | solution.py:91
  427.0 295.0 %copy-start.1 = (bf16[1,320,2048]{2,1,0:T(8,128)(2,1)S(1)}, bf16[1,320,2048]{2,1,0:T(8,128)(2,1)}, u32[]{:S(2)}) copy-start(bf16[1,320,2048]{2,1,0:T(8,128)(2,1)} %param.10) | copy-start | bytes 3932164
Sparse Core Ops, SparseCore 0:
  10.6 86.5 all-gather.2
  99.8 82.2 all-gather.4
  201.5 215.5 reduce-scatter.4
  419.4 65.5 all-reduce.2
  488.9 231.3 reduce-scatter.2
where the time goes:
time: 733 us; the launch traced here: 729 us
  waiting for transfers between devices  574 us (78%)
  matrix products  44.2 us (6%)
  local copies, waits for them, and re-layouts  41.1 us (6%)
  other arithmetic  34.1 us (5%)
  blocking collectives  20.4 us (3%)
  between operations  14.5 us (2%)
    reduce_scatter x1, waiting for transfers between devices, on_device(): lax.psum_scatter(jnp.concatenate([key_grad, value_grad], axis=1).astype(j...  234 us
    reduce_scatter x1, waiting for transfers between devices, on_device(): lax.psum_scatter(weight_part.astype(jnp.bfloat16), 'ctx', scatter_dimensi...  178 us
    all_gather x1, waiting for transfers between devices, on_device(): lax.all_gather(values, 'ctx', axis=1, tiled=True)  68.7 us
    psum x1, waiting for transfers between devices, on_device(): d_weight = lax.psum(column_sum, 'dp').astype(jnp.float32)  51.6 us
    all_gather x1, waiting for transfers between devices, on_device(): lax.all_gather(keys, 'ctx', axis=1, tiled=True)  40.4 us
    lt x1, other arithmetic, on_device(): every_slot % cap_rows  20.9 us
    unnamed x1, blocking collectives  20.4 us
  transfers between devices with their start and end apart: 5, of which 5 were waited for; matrix products, arithmetic and copies ran while one was open for 13% of the time, Pallas kernels for 0%

commit v1 on v0

v1 whole, which is shorter than its diff:
```python
import functools
import math

import jax
import jax.numpy as jnp
from jax import lax
from jax.experimental import pallas as pl
from jax.experimental.pallas import tpu as pltpu
from jax.sharding import PartitionSpec as P

MESH = pl.DeviceIdType.MESH
HD = 128
CORES = 2
NEG = -1e30
F32 = jnp.float32
BF16 = jnp.bfloat16


def rows_dot(a, b):
    return lax.dot_general(a, b, (((1,), (1,)), ((), ())), preferred_element_type=F32)


def dot(a, b):
    return jnp.dot(a, b, preferred_element_type=F32)


def turned(a):
    return jnp.transpose(a.astype(F32)).astype(a.dtype)


def kernel(
    dims,
    grad_hbm, chosen_ref, counts_ref, q_hbm, k_hbm, v_hbm, logit_ref, w_hbm,
    dq_hbm, dk_hbm, dv_hbm, dlogit_ref, dw_ref,
    grad_v, w_v, own_v, got_v, far_v, kb_v, kc_v, vc_v, qc_v, qb_v,
    d_all, da_send, da_v, s_v, p_v, m_v, a_v, dan_v, dl_send, dl_got, c_v, delta_v,
    ds_v, dq_acc, dq_send, part_send, part_got, own_dk, own_dv, dkv_send,
    a_all, t_send, t_got, t_own, z_send, z_got, w_all,
    load_sem, big_sem, send1, recv1, fsend, frecv, dasend, darecv, dsend, drecv,
    asend, arecv, lsend, lrecv, psend, precv, qsend, qrecv, kvsend, kvrecv,
    tsend, trecv, zsend, zrecv, wsend, wrecv,
):
    DP, Y, Z, CAP, PB = dims
    X = DP // CORES
    NQ = Z * CAP
    NB = Z // PB
    BR = PB * CAP
    dp = lax.axis_index("dp")
    ctx = lax.axis_index("ctx")
    y = lax.div(ctx, Z)
    z = lax.rem(ctx, Z)
    x = lax.div(dp, CORES)
    core = lax.rem(dp, CORES)
    width = Z * HD
    model = w_v.shape[1]
    cols_y = model // Y
    cols = cols_y // Z
    scale = 1.0 / math.sqrt(HD)
    c2 = scale * math.log2(math.e)

    def at(yy, zz):
        return yy * Z + zz

    def remote(src, dst, ss, rs, to_dp, to_ctx):
        return pltpu.make_async_remote_copy(
            src_ref=src, dst_ref=dst, send_sem=ss, recv_sem=rs,
            device_id=(to_dp, to_ctx), device_id_type=MESH,
        )

    def arrived(dst, rs):
        remote(dst, dst, rs, rs, dp, ctx).wait_recv()

    def left(src, ss):
        remote(src, src, ss, ss, dp, ctx).wait_send()

    def offset(i):
        half = lax.div(i + 1, 2)
        odd = lax.rem(i, 2)
        return odd * half + (1 - odd) * lax.rem(Z - half, Z)

    def head_cols(h):
        return pl.ds(pl.multiple_of(h * HD, HD), HD)

    barrier = pltpu.get_barrier_semaphore()

    def greet(to_dp, to_ctx):
        pl.semaphore_signal(barrier, inc=1, device_id=(to_dp, to_ctx), device_id_type=MESH)

    @pl.loop(1, Z)
    def _(i):
        greet(dp, at(y, lax.rem(z + i, Z)))

    @pl.loop(1, Y)
    def _(i):
        greet(dp, at(lax.rem(y + i, Y), z))

    @pl.loop(1, DP)
    def _(i):
        greet(lax.rem(dp + i, DP), ctx)

    @pl.loop(0, DP)
    def _(s):
        @pl.when(jnp.logical_not((s == dp) & (z == dp)))
        def _():
            greet(s, at(y, dp))

    @pl.loop(0, Z)
    def _(h):
        pltpu.make_async_copy(k_hbm.at[0, :, head_cols(h)], own_v.at[h, pl.ds(0, CAP)], load_sem.at[0, h]).start()
        pltpu.make_async_copy(v_hbm.at[0, :, head_cols(h)], own_v.at[h, pl.ds(CAP, CAP)], load_sem.at[1, h]).start()
        pltpu.make_async_copy(
            q_hbm.at[0, :, head_cols(h)], own_v.at[h, pl.ds(2 * CAP + 16, CAP)], load_sem.at[2, h]
        ).start()

    pltpu.make_async_copy(grad_hbm.at[0], grad_v, big_sem.at[0]).start()
    pltpu.make_async_copy(w_hbm, w_v, big_sem.at[1]).start()
    count = counts_ref[0, 0].astype(F32)

    @pl.loop(0, Z)
    def _(h):
        own_v[h, pl.ds(2 * CAP, 16), :] = jnp.full((16, HD), count, F32).astype(BF16)

    @pl.loop(0, Z)
    def _(h):
        for which, first in ((0, 0), (1, CAP), (2, 2 * CAP + 16)):
            pltpu.make_async_copy(
                q_hbm.at[0, :, head_cols(h)], own_v.at[h, pl.ds(first, CAP)], load_sem.at[which, h]
            ).wait()

    pl.semaphore_wait(barrier, (Z - 1) + (Y - 1) + (DP - 1) + DP - (dp == z).astype(jnp.int32))

    @pl.loop(1, Z)
    def _(i):
        to = lax.rem(z + offset(i), Z)
        remote(own_v.at[to], got_v.at[z], send1.at[to], recv1.at[z], dp, at(y, to)).start()

    pltpu.make_async_copy(own_v.at[z], got_v.at[z], recv1.at[z]).start()

    eye = lax.broadcasted_iota(jnp.int32, (CAP, CAP), 0) == lax.broadcasted_iota(jnp.int32, (CAP, CAP), 1)

    def column(row):
        return jnp.sum(jnp.where(eye, row, 0.0), axis=1, keepdims=True)

    gate_row = jax.nn.sigmoid(logit_ref[...])
    live_col = lax.broadcasted_iota(jnp.int32, (CAP, 1), 0).astype(F32) < count
    chosen_col = column(chosen_ref[...].astype(F32))
    toks = grad_v.shape[0]
    hot = jnp.where(
        (lax.broadcasted_iota(jnp.int32, (CAP, toks), 1).astype(F32) == chosen_col) & live_col, 1.0, 0.0
    ).astype(BF16)
    gate_col = column(gate_row)
    pltpu.make_async_copy(grad_hbm.at[0], grad_v, big_sem.at[0]).wait()
    half = model // 2

    @pl.loop(0, 2)
    def _(i):
        part = pl.ds(pl.multiple_of(i * half, HD), half)
        d_all[dp, :, part] = (gate_col * dot(hot, grad_v[:, part])).astype(BF16)

    @pl.loop(1, X)
    def _(i):
        to = lax.rem(x + i, X) * CORES + core
        remote(d_all.at[dp], d_all.at[dp], dsend.at[i], drecv.at[dp], to, ctx).start()

    other = x * CORES + (1 - core)
    remote(d_all.at[dp], d_all.at[dp], dsend.at[0], drecv.at[dp], other, ctx).start()

    lane = lax.broadcasted_iota(jnp.int32, (1, NQ), 1).astype(F32)

    def live_lanes(zz, cnt):
        base = (zz * CAP).astype(F32)
        return (lane >= base) & (lane - base < cnt)

    def later_y(i):
        return y + i < Y

    pltpu.make_async_copy(w_hbm, w_v, big_sem.at[1]).wait()

    def step(i, kb):
        off = offset(i)
        to = lax.rem(z + off, Z)
        frm = lax.rem(z + Z - off, Z)
        w_h = w_v[pl.ds(pl.multiple_of(to * HD, HD), HD), :]
        da = rows_dot(d_all[dp], w_h).astype(BF16)
        da_send[to] = da

        @pl.when(i > 0)
        def _():
            remote(da_send.at[to], da_v.at[z], dasend.at[to], darecv.at[z], dp, at(y, to)).start()

        @pl.when(i == 0)
        def _():
            da_v[z] = da

        arrived(got_v.at[frm], recv1.at[frm])

        @pl.loop(1, Y)
        def _(j):
            @pl.when(later_y(j))
            def _():
                kv = pl.ds(0, 2 * CAP + 16)
                remote(
                    got_v.at[frm, kv], far_v.at[j - 1, frm], fsend.at[j - 1, frm], frecv.at[j - 1, frm],
                    dp, at(y + j, z),
                ).start()

        kc_v[0, frm] = got_v[frm, pl.ds(0, CAP), :]
        vc_v[0, frm] = got_v[frm, pl.ds(CAP, CAP), :]
        qc_v[frm] = got_v[frm, pl.ds(2 * CAP + 16, CAP), :]
        cnt = got_v[frm, pl.ds(2 * CAP, 16), :].astype(F32)[0:1, 0:1]
        rows = lax.broadcasted_iota(jnp.int32, (CAP, 1), 0).astype(F32)
        qb_v[frm] = jnp.where(rows < cnt, 0.0, NEG)
        return jnp.where(live_lanes(frm, cnt), 0.0, kb)

    kb0 = lax.fori_loop(0, Z, step, jnp.full((1, NQ), NEG, F32))
    kb_v[0] = jnp.broadcast_to(kb0, (8, NQ))

    def flat(a):
        return a.reshape(a.shape[0] * a.shape[1], a.shape[2])

    def blocks(a):
        return a.reshape(PB, CAP, a.shape[1])

    @pl.loop(0, NB)
    def _(b):
        some = pl.ds(b * PB, PB)
        s = rows_dot(flat(qc_v[some]), flat(kc_v[0]))
        qb = flat(qb_v[some])
        row = lax.broadcasted_iota(jnp.int32, (BR, NQ), 0) + b * BR
        col = lax.broadcasted_iota(jnp.int32, (BR, NQ), 1)
        masked = jnp.where(col < row, s + kb_v[0, 0:1, :] + qb, NEG)
        s = jnp.where(col == row, s, masked)
        s_v[0, some] = blocks(s)
        m_v[some] = blocks(jnp.max(s, axis=1, keepdims=True))

    def earlier(d, _):
        @pl.loop(0, Z)
        def _(zz):
            arrived(far_v.at[d - 1, zz], frecv.at[d - 1, zz])

        def bring(zz, kb):
            kc_v[d, zz] = far_v[d - 1, zz, pl.ds(0, CAP), :]
            vc_v[d, zz] = far_v[d - 1, zz, pl.ds(CAP, CAP), :]
            cnt = far_v[d - 1, zz, pl.ds(2 * CAP, 16), :].astype(F32)[0:1, 0:1]
            return jnp.where(live_lanes(zz, cnt), 0.0, kb)

        kb = lax.fori_loop(0, Z, bring, jnp.full((1, NQ), NEG, F32))

        @pl.loop(0, NB)
        def _(b):
            some = pl.ds(b * PB, PB)
            s = rows_dot(flat(qc_v[some]), flat(kc_v[d])) + kb
            s_v[d, some] = blocks(s)
            top = jnp.max(s, axis=1, keepdims=True) + flat(qb_v[some])
            m_v[some] = blocks(jnp.maximum(flat(m_v[some]), top))

        return 0

    lax.fori_loop(1, y + 1, earlier, 0)

    @pl.loop(1, X)
    def _(i):
        frm = lax.rem(x + i, X) * CORES + core
        arrived(d_all.at[frm], drecv.at[frm])
        remote(d_all.at[frm], d_all.at[frm], dsend.at[X - 1 + i], drecv.at[frm], other, ctx).start()

    @pl.loop(1, Z)
    def _(i):
        frm = lax.rem(z + i, Z)
        arrived(da_v.at[frm], darecv.at[frm])

    wide = lax.broadcasted_iota(jnp.int32, (CAP, HD), 0) == lax.broadcasted_iota(jnp.int32, (CAP, HD), 1)

    @pl.loop(0, NB)
    def _(b):
        some = pl.ds(b * PB, PB)
        mc = flat(m_v[some]) * c2
        qb = flat(qb_v[some])

        def one(d, carry):
            total, o = carry
            top = mc - jnp.where(d > 0, qb, 0.0)
            p = jnp.exp2(flat(s_v[d, some]) * c2 - top)
            pb = p.astype(BF16)
            p_v[d, some] = blocks(pb)
            return total + jnp.sum(p, axis=1, keepdims=True), o + dot(pb, flat(vc_v[d]))

        total, o = lax.fori_loop(0, y + 1, one, (jnp.zeros((BR, 1), F32), jnp.zeros((BR, HD), F32)))
        inv = 1.0 / total
        att = (o * inv).astype(BF16)
        a_v[some] = blocks(att)
        da = flat(da_v[some]).astype(F32)
        delta = jnp.sum(da * att.astype(F32), axis=1, keepdims=True)
        delta_v[some] = blocks(delta)
        c_v[some] = blocks(inv * scale)
        dan_v[some] = blocks((da * inv).astype(BF16))
        for k in range(PB):
            mine = delta[k * CAP : (k + 1) * CAP]
            row = jnp.sum(jnp.where(wide, mine, 0.0), axis=0, keepdims=True)
            dl_send[b * PB + k] = jnp.broadcast_to(row, (8, HD))

    @pl.loop(0, Z)
    def _(i):
        to = lax.rem(z + i, Z)

        @pl.when(jnp.logical_not((dp == z) & (i == 0)))
        def _():
            remote(a_v.at[to], a_all.at[dp], asend.at[to], arecv.at[dp], z, at(y, to)).start()

        @pl.when(i > 0)
        def _():
            remote(dl_send.at[to], dl_got.at[z], lsend.at[to], lrecv.at[z], dp, at(y, to)).start()

    @pl.when(dp == z)
    def _():
        a_all[dp] = a_v[z]

    dl_got[z] = dl_send[z]

    q_t = turned(flat(qc_v[...]))
    da_t = turned(flat(dan_v[...]))
    dq_acc[...] = jnp.zeros_like(dq_acc)

    def backward(d):
        @pl.loop(0, NB)
        def _(b):
            some = pl.ds(b * PB, PB)
            dprobs = rows_dot(flat(da_v[some]), flat(vc_v[d]))
            ds = flat(p_v[d, some]).astype(F32) * ((dprobs - flat(delta_v[some])) * flat(c_v[some]))
            ds = ds.astype(BF16)
            ds_v[some] = blocks(ds)
            dq_acc[some] += blocks(dot(ds, flat(kc_v[d])))

        dk_t = dot(q_t, flat(ds_v[...]))
        dv_t = dot(da_t, flat(p_v[d]))
        return jnp.transpose(dk_t), jnp.transpose(dv_t)

    def pieces(a):
        return a.reshape(Z, CAP, HD)

    def far(i, _):
        d = y + 1 - i
        dk, dv = backward(d)
        part_send[d - 1, 0] = pieces(dk.astype(BF16))
        part_send[d - 1, 1] = pieces(dv.astype(BF16))
        remote(
            part_send.at[d - 1], part_got.at[d - 1], psend.at[d - 1], precv.at[d - 1], dp, at(y - d, z)
        ).start()
        return 0

    lax.fori_loop(1, y + 1, far, 0)

    @pl.loop(0, DP)
    def _(s):
        @pl.when(jnp.logical_not((s == dp) & (z == dp)))
        def _():
            arrived(a_all.at[s], arecv.at[s])

    @pl.loop(0, X)
    def _(i):
        frm = lax.rem(x + i, X) * CORES + 1 - core
        arrived(d_all.at[frm], drecv.at[frm])

    a_t = turned(flat(a_all[...]))

    @pl.loop(1, Y + 1)
    def _(i):
        to = lax.rem(y + i, Y)
        t = dot(a_t, flat(d_all[:, :, pl.ds(pl.multiple_of(to * cols_y, HD), cols_y)]))

        @pl.when(i < Y)
        def _():
            t_send[i - 1] = t.astype(BF16)
            remote(t_send.at[i - 1], t_got.at[i - 1], tsend.at[i - 1], trecv.at[i - 1], dp, at(to, z)).start()

        @pl.when(i == Y)
        def _():
            t_own[...] = t

    dk, dv = backward(0)
    own_dk[...] = pieces(dk)
    own_dv[...] = pieces(dv)
    dq_send[...] = dq_acc[...].astype(BF16)

    @pl.loop(0, Z)
    def _(i):
        to = lax.rem(z + i, Z)

        @pl.when(i > 0)
        def _():
            remote(dq_send.at[to], dq_hbm.at[0, :, head_cols(z)], qsend.at[to], qrecv.at[z], dp, at(y, to)).start()

        @pl.when(i == 0)
        def _():
            pltpu.make_async_copy(dq_send.at[z], dq_hbm.at[0, :, head_cols(z)], qrecv.at[z]).start()

    @pl.loop(0, Y - 1)
    def _(i):
        arrived(t_got.at[i], trecv.at[i])

    t_all = t_own[...]
    for i in range(Y - 1):
        t_all = t_all + t_got[i].astype(F32)
    z_send[...] = jnp.transpose(t_all).astype(BF16).reshape(Z, cols, HD)

    @pl.loop(1, Z)
    def _(i):
        to = lax.rem(z + i, Z)
        remote(z_send.at[to], z_got.at[z], zsend.at[to], zrecv.at[z], dp, at(y, to)).start()

    z_got[z] = z_send[z]

    def add(d, _):
        arrived(part_got.at[d - 1], precv.at[d - 1])
        own_dk[...] += part_got[d - 1, 0].astype(F32)
        own_dv[...] += part_got[d - 1, 1].astype(F32)
        return 0

    lax.fori_loop(1, Y - y, add, 0)
    dkv_send[0] = own_dk[...].astype(BF16)
    dkv_send[1] = own_dv[...].astype(BF16)

    @pl.loop(0, Z)
    def _(i):
        to = lax.rem(z + i, Z)
        for which, out in ((0, dk_hbm), (1, dv_hbm)):

            @pl.when(i > 0)
            def _():
                remote(
                    dkv_send.at[which, to], out.at[0, :, head_cols(z)], kvsend.at[which, to], kvrecv.at[which, z],
                    dp, at(y, to),
                ).start()

            @pl.when(i == 0)
            def _():
                pltpu.make_async_copy(
                    dkv_send.at[which, z], out.at[0, :, head_cols(z)], kvrecv.at[which, z]
                ).start()

    @pl.loop(1, Z)
    def _(i):
        frm = lax.rem(z + i, Z)
        arrived(z_got.at[frm], zrecv.at[frm])

    tile = z_got[0].astype(F32)
    for i in range(1, Z):
        tile = tile + z_got[i].astype(F32)
    w_all[dp] = tile

    @pl.loop(1, DP)
    def _(i):
        to = lax.rem(dp + i, DP)
        remote(w_all.at[dp], w_all.at[dp], wsend.at[i], wrecv.at[dp], to, ctx).start()

    @pl.loop(1, Z)
    def _(i):
        frm = lax.rem(z + i, Z)
        arrived(dl_got.at[frm], lrecv.at[frm])

    delta_sum = dl_got[0]
    for i in range(1, Z):
        delta_sum = delta_sum + dl_got[i]
    live_row = lax.broadcasted_iota(jnp.int32, (1, CAP), 1).astype(F32) < count
    dlogit_ref[...] = jnp.where(live_row, (1.0 - gate_row) * delta_sum[0:1, 0:CAP], 0.0)

    @pl.loop(1, DP)
    def _(i):
        frm = lax.rem(dp + i, DP)
        arrived(w_all.at[frm], wrecv.at[frm])

    for h in range(DP):
        dw_ref[pl.ds(h * HD, HD), :] = jnp.transpose(w_all[h])

    @pl.loop(0, Z)
    def _(i):
        arrived(dq_hbm.at[0, :, head_cols(i)], qrecv.at[i])
        arrived(dk_hbm.at[0, :, head_cols(i)], kvrecv.at[0, i])
        arrived(dv_hbm.at[0, :, head_cols(i)], kvrecv.at[1, i])

    @pl.loop(1, Z)
    def _(i):
        to = lax.rem(z + i, Z)
        left(own_v.at[to], send1.at[to])
        left(da_send.at[to], dasend.at[to])
        left(dl_send.at[to], lsend.at[to])
        left(dq_send.at[to], qsend.at[to])
        left(z_send.at[to], zsend.at[to])
        left(dkv_send.at[0, to], kvsend.at[0, to])
        left(dkv_send.at[1, to], kvsend.at[1, to])

    @pl.loop(0, Z)
    def _(i):
        to = lax.rem(z + i, Z)

        @pl.when(jnp.logical_not((dp == z) & (i == 0)))
        def _():
            left(a_v.at[to], asend.at[to])

    @pl.loop(0, 2 * X - 1)
    def _(i):
        left(d_all.at[dp], dsend.at[i])

    @pl.loop(1, Y)
    def _(j):
        left(t_send.at[j - 1], tsend.at[j - 1])

        @pl.when(later_y(j))
        def _():
            @pl.loop(0, Z)
            def _(zz):
                left(far_v.at[j - 1, zz], fsend.at[j - 1, zz])

        @pl.when(y >= j)
        def _():
            left(part_send.at[j - 1], psend.at[j - 1])

    @pl.loop(1, DP)
    def _(i):
        left(w_all.at[dp], wsend.at[i])


def solution(mesh, y_extent=4, block=2):
    dp_n, ctx_n = mesh.shape["dp"], mesh.shape["ctx"]
    z_n = ctx_n // y_extent

    def on_device(grad_out, chosen, counts, queries, keys, values, router_logit, out_weight):
        cap, width = queries.shape[1:]
        toks, model = grad_out.shape[1:]
        nq = z_n * cap
        y_n = y_extent
        cols_y = model // y_n
        cols = cols_y // z_n
        assert width == z_n * HD == dp_n * HD
        vm = pltpu.VMEM
        dma = pltpu.SemaphoreType.DMA
        scratch = [
            vm((toks, model), BF16),
            vm((width, model), BF16),
            vm((z_n, 3 * cap + 16, HD), BF16),
            vm((z_n, 3 * cap + 16, HD), BF16),
            vm((y_n - 1, z_n, 2 * cap + 16, HD), BF16),
            vm((1, 8, nq), F32),
            vm((y_n, z_n, cap, HD), BF16),
            vm((y_n, z_n, cap, HD), BF16),
            vm((z_n, cap, HD), BF16),
            vm((z_n, cap, 1), F32),
            vm((dp_n, cap, model), BF16),
            vm((z_n, cap, HD), BF16),
            vm((z_n, cap, HD), BF16),
            vm((y_n, z_n, cap, nq), F32),
            vm((y_n, z_n, cap, nq), BF16),
            vm((z_n, cap, 1), F32),
            vm((z_n, cap, HD), BF16),
            vm((z_n, cap, HD), BF16),
            vm((z_n, 8, HD), F32),
            vm((z_n, 8, HD), F32),
            vm((z_n, cap, 1), F32),
            vm((z_n, cap, 1), F32),
            vm((z_n, cap, nq), BF16),
            vm((z_n, cap, HD), F32),
            vm((z_n, cap, HD), BF16),
            vm((y_n - 1, 2, z_n, cap, HD), BF16),
            vm((y_n - 1, 2, z_n, cap, HD), BF16),
            vm((z_n, cap, HD), F32),
            vm((z_n, cap, HD), F32),
            vm((2, z_n, cap, HD), BF16),
            vm((dp_n, cap, HD), BF16),
            vm((y_n - 1, HD, cols_y), BF16),
            vm((y_n - 1, HD, cols_y), BF16),
            vm((HD, cols_y), F32),
            vm((z_n, cols, HD), BF16),
            vm((z_n, cols, HD), BF16),
            vm((dp_n, cols, HD), F32),
            dma((3, z_n)),
            dma((2,)),
            dma((z_n,)), dma((z_n,)),
            dma((y_n - 1, z_n)), dma((y_n - 1, z_n)),
            dma((z_n,)), dma((z_n,)),
            dma((dp_n,)), dma((dp_n,)),
            dma((z_n,)), dma((dp_n,)),
            dma((z_n,)), dma((z_n,)),
            dma((y_n - 1,)), dma((y_n - 1,)),
            dma((z_n,)), dma((z_n,)),
            dma((2, z_n)), dma((2, z_n)),
            dma((y_n - 1,)), dma((y_n - 1,)),
            dma((z_n,)), dma((z_n,)),
            dma((dp_n,)), dma((dp_n,)),
        ]
        hbm = pl.BlockSpec(memory_space=pl.ANY)
        vmem = pl.BlockSpec(memory_space=pltpu.VMEM)
        smem = pl.BlockSpec(memory_space=pltpu.SMEM)
        grads = jax.ShapeDtypeStruct((1, cap, width), BF16)
        return pl.pallas_call(
            functools.partial(kernel, (dp_n, y_n, z_n, cap, block)),
            out_shape=(
                grads,
                grads,
                grads,
                jax.ShapeDtypeStruct((1, cap), F32),
                jax.ShapeDtypeStruct((width, model // ctx_n), F32),
            ),
            in_specs=[hbm, vmem, smem, hbm, hbm, hbm, vmem, hbm],
            out_specs=(hbm, hbm, hbm, vmem, vmem),
            scratch_shapes=scratch,
            compiler_params=pltpu.CompilerParams(
                collective_id=0, has_side_effects=True, vmem_limit_bytes=50 * 2**20
            ),
        )(grad_out, chosen, counts, queries, keys, values, router_logit, out_weight)

    return jax.shard_map(
        on_device,
        mesh=mesh,
        in_specs=(
            P("dp", "ctx", None),
            P("dp", "ctx"),
            P("dp", "ctx"),
            P("dp", "ctx", None),
            P("dp", "ctx", None),
            P("dp", "ctx", None),
            P("dp", "ctx"),
            P(),
        ),
        out_specs=(
            P("dp", "ctx", None),
            P("dp", "ctx", None),
            P("dp", "ctx", None),
            P("dp", "ctx"),
            P(None, "ctx"),
        ),
        check_vma=False,
    )
```

time: 733 us -> 87.3 us (0.12)
  the two profiles are of different devices: /device:TPU:1 before, /device:TPU:81 now
where the time goes in v1:
time: 87.3 us; the launch traced here: 87.1 us
  Pallas kernels  77.1 us (88%)
  local copies, waits for them, and re-layouts  8.76 us (10%)
  between operations  1.3 us (1%)
    pallas_call x1, Pallas kernels, on_device(): pl.pallas_call(functools.partial(kernel, (dp_n, y_n, z_n, cap, block)), o...  77.1 us
    unnamed x16, local copies, waits for them, and re-layouts  7.87 us

profile of v1, /device:TPU:81, one launch (start us, length us, event | category | flops | bytes accessed | tf_op | source)
XLA Modules:
  0.0 87.1 jit_solution(4844290787548933780)
XLA Ops:
  1.3 0.0 copy-start
  1.3 1.3 %copy-done = bf16[1,320,2048]{2,1,0:T(8,128)(2,1)S(1)} copy-done((bf16[1,320,2048]{2,1,0:T(8,128)(2,1)S(1)}, bf16[1,320,2048]{2,1,0:T(8,128)(2,1)}, u32[]{:S(2)}) %copy-start) | copy-done | bytes 1310744
  2.6 0.0 copy-start.1
  2.6 0.9 %copy-done.1 = bf16[1,80,1024]{2,1,0:T(8,128)(2,1)S(1)} copy-done((bf16[1,80,1024]{2,1,0:T(8,128)(2,1)S(1)}, bf16[1,80,1024]{2,1,0:T(8,128)(2,1)}, u32[]{:S(2)}) %copy-start.1) | copy-done | bytes 163864
  3.5 0.0 copy-start.2
  3.5 0.9 %copy-done.2 = bf16[1,80,1024]{2,1,0:T(8,128)(2,1)S(1)} copy-done((bf16[1,80,1024]{2,1,0:T(8,128)(2,1)S(1)}, bf16[1,80,1024]{2,1,0:T(8,128)(2,1)}, u32[]{:S(2)}) %copy-start.2) | copy-done | bytes 163864
  4.4 0.0 copy-start.3
  4.4 0.9 %copy-done.3 = bf16[1,80,1024]{2,1,0:T(8,128)(2,1)S(1)} copy-done((bf16[1,80,1024]{2,1,0:T(8,128)(2,1)S(1)}, bf16[1,80,1024]{2,1,0:T(8,128)(2,1)}, u32[]{:S(2)}) %copy-start.3) | copy-done | bytes 163864
  5.3 0.0 copy-start.4
  5.3 0.7 copy-done.4
  6.0 0.0 copy-start.5
  6.0 0.7 copy-done.5
  6.7 77.1 %shard_map.119 = (bf16[1,80,1024]{2,1,0:T(8,128)(2,1)S(1)}, bf16[1,80,1024]{2,1,0:T(8,128)(2,1)S(1)}, bf16[1,80,1024]{2,1,0:T(8,128)(2,1)S(1)}, f32[1,80]{1,0:T(1,128)S(1)}, f32[1024,64]{1,0:T(8,128)S(1)}) custom-call(bf16[1,320,2048]{2,1,0:T(8,128)(2,1)S(1)} %copy-done, s32[1,80]{1,0:T(1,128)S(1)} %copy-done.4, s32[1,1]{1,0:T(1,128)S(6)} %copy.18.counts_ref, ...), custom_call_target="tpu_custom_call" | custom-call | tf_op jit(solution)/shard_map/pallas_call | solution.py:594
  83.7 0.9 %copy.13 = f32[1024,64]{0,1:T(8,128)} copy(f32[1024,64]{1,0:T(8,128)S(1)} %get-tuple-element.9) | data formatting | bytes 524288 | tf_op jit(solution)/shard_map/pallas_call | solution.py:594
  84.6 0.7 copy.19
  85.3 0.7 copy.20
  85.9 0.7 copy.21
  86.6 0.5 copy.22
Async XLA Ops:
  1.3 1.3 %copy-start = (bf16[1,320,2048]{2,1,0:T(8,128)(2,1)S(1)}, bf16[1,320,2048]{2,1,0:T(8,128)(2,1)}, u32[]{:S(2)}) copy-start(bf16[1,320,2048]{2,1,0:T(8,128)(2,1)} %grad_hbm.1) | copy-start | bytes 3932164
  2.6 0.9 %copy-start.1 = (bf16[1,80,1024]{2,1,0:T(8,128)(2,1)S(1)}, bf16[1,80,1024]{2,1,0:T(8,128)(2,1)}, u32[]{:S(2)}) copy-start(bf16[1,80,1024]{2,1,0:T(8,128)(2,1)} %q_hbm.1) | copy-start | bytes 491524
  3.5 0.9 %copy-start.2 = (bf16[1,80,1024]{2,1,0:T(8,128)(2,1)S(1)}, bf16[1,80,1024]{2,1,0:T(8,128)(2,1)}, u32[]{:S(2)}) copy-start(bf16[1,80,1024]{2,1,0:T(8,128)(2,1)} %k_hbm.1) | copy-start | bytes 491524
  4.4 0.9 %copy-start.3 = (bf16[1,80,1024]{2,1,0:T(8,128)(2,1)S(1)}, bf16[1,80,1024]{2,1,0:T(8,128)(2,1)}, u32[]{:S(2)}) copy-start(bf16[1,80,1024]{2,1,0:T(8,128)(2,1)} %v_hbm.1) | copy-start | bytes 491524
  5.3 0.7 copy-start.4
  6.0 0.7 copy-start.5

commit v2 on v1

v2 whole, which is shorter than its diff:
```python
import functools
import math

import jax
import jax.numpy as jnp
from jax import lax
from jax.experimental import pallas as pl
from jax.experimental.pallas import tpu as pltpu
from jax.sharding import PartitionSpec as P

MESH = pl.DeviceIdType.MESH
HD = 128
CORES = 2
NEG = -1e30
F32 = jnp.float32
BF16 = jnp.bfloat16


def rows_dot(a, b):
    return lax.dot_general(a, b, (((1,), (1,)), ((), ())), preferred_element_type=F32)


def dot(a, b):
    return jnp.dot(a, b, preferred_element_type=F32)


def turned(a):
    return jnp.transpose(a.astype(F32)).astype(a.dtype)


def kernel(
    dims,
    grad_hbm, chosen_hbm, counts_hbm, q_hbm, k_hbm, v_hbm, logit_hbm, w_hbm,
    dq_hbm, dkv_hbm, dlogit_ref, dw_ref,
    chosen_ref, counts_ref, logit_ref, q_in, k_in, v_in,
    grad_v, w_v, own_v, got_v, far_v, kb_v, kc_v, vc_v, qc_v, qb_v,
    d_all, da_send, da_v, s_v, p_v, m_v, a_v, dan_v, dl_send, dl_got, c_v, delta_v,
    ds_v, dq_acc, dq_send, part_send, part_got, own_dk, own_dv, dkv_send,
    a_all, t_send, t_got, t_own, z_send, z_got, w_all,
    load_sem, send1, recv1, fsend, frecv, dasend, darecv, dsend, drecv, d2recv,
    asend, arecv, lsend, lrecv, psend, precv, qsend, qrecv, kvsend, kvrecv,
    tsend, trecv, zsend, zrecv, wsend, wrecv,
):
    DP, Y, Z, CAP, PB = dims
    X = DP // CORES
    NQ = Z * CAP
    NB = Z // PB
    BR = PB * CAP
    dp = lax.axis_index("dp")
    ctx = lax.axis_index("ctx")
    y = lax.div(ctx, Z)
    z = lax.rem(ctx, Z)
    x = lax.div(dp, CORES)
    core = lax.rem(dp, CORES)
    width = Z * HD
    model = w_v.shape[1]
    cols_y = model // Y
    cols = cols_y // Z
    scale = 1.0 / math.sqrt(HD)
    c2 = scale * math.log2(math.e)

    def at(yy, zz):
        return yy * Z + zz

    def remote(src, dst, ss, rs, to_dp, to_ctx):
        return pltpu.make_async_remote_copy(
            src_ref=src, dst_ref=dst, send_sem=ss, recv_sem=rs,
            device_id=(to_dp, to_ctx), device_id_type=MESH,
        )

    def arrived(dst, rs):
        remote(dst, dst, rs, rs, dp, ctx).wait_recv()

    def left(src, ss):
        remote(src, src, ss, ss, dp, ctx).wait_send()

    def offset(i):
        half = lax.div(i + 1, 2)
        odd = lax.rem(i, 2)
        return odd * half + (1 - odd) * lax.rem(Z - half, Z)

    def head_cols(h):
        return pl.ds(pl.multiple_of(h * HD, HD), HD)

    loads = [
        (counts_hbm, counts_ref), (chosen_hbm, chosen_ref), (logit_hbm, logit_ref),
        (k_hbm.at[0], k_in), (v_hbm.at[0], v_in), (q_hbm.at[0], q_in), (grad_hbm.at[0], grad_v), (w_hbm, w_v),
    ]

    def load(i):
        return pltpu.make_async_copy(loads[i][0], loads[i][1], load_sem.at[i])

    for i in range(len(loads)):
        load(i).start()

    barrier = pltpu.get_barrier_semaphore()

    def greet(to_dp, to_ctx):
        pl.semaphore_signal(barrier, inc=1, device_id=(to_dp, to_ctx), device_id_type=MESH)

    @pl.loop(1, Z)
    def _(i):
        greet(dp, at(y, lax.rem(z + i, Z)))

    @pl.loop(1, Y)
    def _(i):
        greet(dp, at(lax.rem(y + i, Y), z))

    @pl.loop(1, DP)
    def _(i):
        greet(lax.rem(dp + i, DP), ctx)

    @pl.loop(0, DP)
    def _(s):
        @pl.when(jnp.logical_not((s == dp) & (z == dp)))
        def _():
            greet(s, at(y, dp))

    for i in range(6):
        load(i).wait()
    count = counts_ref[...].astype(F32)
    meta = jnp.broadcast_to(count, (16, HD)).astype(BF16)
    for h in range(Z):
        cut = pl.ds(h * HD, HD)
        own_v[h, pl.ds(0, CAP), :] = k_in[:, cut]
        own_v[h, pl.ds(CAP, CAP), :] = v_in[:, cut]
        own_v[h, pl.ds(2 * CAP, 16), :] = meta
        own_v[h, pl.ds(2 * CAP + 16, CAP), :] = q_in[:, cut]

    eye = lax.broadcasted_iota(jnp.int32, (CAP, CAP), 0) == lax.broadcasted_iota(jnp.int32, (CAP, CAP), 1)

    def column(row):
        return jnp.sum(jnp.where(eye, row, 0.0), axis=1, keepdims=True)

    gate_row = jax.nn.sigmoid(logit_ref[...])
    live_col = lax.broadcasted_iota(jnp.int32, (CAP, 1), 0).astype(F32) < count
    chosen_col = column(chosen_ref[...].astype(F32))
    toks = grad_v.shape[0]
    hot = jnp.where(
        (lax.broadcasted_iota(jnp.int32, (CAP, toks), 1).astype(F32) == chosen_col) & live_col, 1.0, 0.0
    ).astype(BF16)
    gate_col = column(gate_row)
    load(6).wait()
    d_all[dp] = (gate_col * dot(hot, grad_v[...])).astype(BF16)

    pl.semaphore_wait(barrier, (Z - 1) + (Y - 1) + (DP - 1) + DP - (dp == z).astype(jnp.int32))

    @pl.loop(1, Z)
    def _(i):
        to = lax.rem(z + offset(i), Z)
        remote(own_v.at[to], got_v.at[z], send1, recv1.at[z], dp, at(y, to)).start()

    pltpu.make_async_copy(own_v.at[z], got_v.at[z], recv1.at[z]).start()

    other = x * CORES + (1 - core)
    remote(d_all.at[dp], d_all.at[dp], dsend, d2recv, other, ctx).start()

    @pl.loop(1, X)
    def _(i):
        to = lax.rem(x + i, X) * CORES + core
        remote(d_all.at[dp], d_all.at[dp], dsend, drecv.at[dp], to, ctx).start()

    load(7).wait()
    da_all = rows_dot(d_all[dp], w_v[...]).astype(BF16)
    for h in range(Z):
        da_send[h] = da_all[:, h * HD : (h + 1) * HD]

    @pl.loop(1, Z)
    def _(i):
        to = lax.rem(z + offset(i), Z)
        remote(da_send.at[to], da_v.at[z], dasend, darecv, dp, at(y, to)).start()

    pltpu.make_async_copy(da_send.at[z], da_v.at[z], darecv).start()

    lane = lax.broadcasted_iota(jnp.int32, (1, NQ), 1).astype(F32)

    def live_lanes(zz, cnt):
        base = (zz * CAP).astype(F32)
        return (lane >= base) & (lane - base < cnt)

    def later_y(i):
        return y + i < Y

    def step(i, kb):
        frm = lax.rem(z + Z - offset(i), Z)
        arrived(got_v.at[frm], recv1.at[frm])

        @pl.loop(1, Y)
        def _(j):
            @pl.when(later_y(j))
            def _():
                kv = pl.ds(0, 2 * CAP + 16)
                remote(
                    got_v.at[frm, kv], far_v.at[j - 1, frm], fsend.at[j - 1], frecv.at[j - 1], dp, at(y + j, z)
                ).start()

        kc_v[0, frm] = got_v[frm, pl.ds(0, CAP), :]
        vc_v[0, frm] = got_v[frm, pl.ds(CAP, CAP), :]
        qc_v[frm] = got_v[frm, pl.ds(2 * CAP + 16, CAP), :]
        cnt = got_v[frm, pl.ds(2 * CAP, 16), :].astype(F32)[0:1, 0:1]
        rows = lax.broadcasted_iota(jnp.int32, (CAP, 1), 0).astype(F32)
        qb_v[frm] = jnp.where(rows < cnt, 0.0, NEG)
        return jnp.where(live_lanes(frm, cnt), 0.0, kb)

    kb0 = lax.fori_loop(0, Z, step, jnp.full((1, NQ), NEG, F32))
    kb_v[0] = jnp.broadcast_to(kb0, (8, NQ))

    def flat(a):
        return a.reshape(a.shape[0] * a.shape[1], a.shape[2])

    def blocks(a):
        return a.reshape(PB, CAP, a.shape[1])

    @pl.loop(0, NB)
    def _(b):
        some = pl.ds(b * PB, PB)
        s = rows_dot(flat(qc_v[some]), flat(kc_v[0]))
        qb = flat(qb_v[some])
        row = lax.broadcasted_iota(jnp.int32, (BR, NQ), 0) + b * BR
        col = lax.broadcasted_iota(jnp.int32, (BR, NQ), 1)
        masked = jnp.where(col < row, s + kb_v[0, 0:1, :] + qb, NEG)
        s = jnp.where(col == row, s, masked)
        s_v[0, some] = blocks(s)
        m_v[some] = blocks(jnp.max(s, axis=1, keepdims=True))

    def earlier(d, _):
        arrived(far_v.at[d - 1], frecv.at[d - 1])

        def bring(zz, kb):
            kc_v[d, zz] = far_v[d - 1, zz, pl.ds(0, CAP), :]
            vc_v[d, zz] = far_v[d - 1, zz, pl.ds(CAP, CAP), :]
            cnt = far_v[d - 1, zz, pl.ds(2 * CAP, 16), :].astype(F32)[0:1, 0:1]
            return jnp.where(live_lanes(zz, cnt), 0.0, kb)

        kb = lax.fori_loop(0, Z, bring, jnp.full((1, NQ), NEG, F32))

        @pl.loop(0, NB)
        def _(b):
            some = pl.ds(b * PB, PB)
            s = rows_dot(flat(qc_v[some]), flat(kc_v[d])) + kb
            s_v[d, some] = blocks(s)
            top = jnp.max(s, axis=1, keepdims=True) + flat(qb_v[some])
            m_v[some] = blocks(jnp.maximum(flat(m_v[some]), top))

        return 0

    lax.fori_loop(1, y + 1, earlier, 0)

    @pl.loop(1, X)
    def _(i):
        frm = lax.rem(x + i, X) * CORES + core
        arrived(d_all.at[frm], drecv.at[frm])
        remote(d_all.at[frm], d_all.at[frm], dsend, d2recv, other, ctx).start()

    arrived(da_v, darecv)

    wide = lax.broadcasted_iota(jnp.int32, (CAP, HD), 0) == lax.broadcasted_iota(jnp.int32, (CAP, HD), 1)

    @pl.loop(0, NB)
    def _(b):
        some = pl.ds(b * PB, PB)
        mc = flat(m_v[some]) * c2
        qb = flat(qb_v[some])

        def one(d, carry):
            total, o = carry
            top = mc - jnp.where(d > 0, qb, 0.0)
            p = jnp.exp2(flat(s_v[d, some]) * c2 - top)
            pb = p.astype(BF16)
            p_v[d, some] = blocks(pb)
            return total + jnp.sum(p, axis=1, keepdims=True), o + dot(pb, flat(vc_v[d]))

        total, o = lax.fori_loop(0, y + 1, one, (jnp.zeros((BR, 1), F32), jnp.zeros((BR, HD), F32)))
        inv = 1.0 / total
        att = (o * inv).astype(BF16)
        a_v[some] = blocks(att)
        da = flat(da_v[some]).astype(F32)
        delta = jnp.sum(da * att.astype(F32), axis=1, keepdims=True)
        delta_v[some] = blocks(delta)
        c_v[some] = blocks(inv * scale)
        dan_v[some] = blocks((da * inv).astype(BF16))
        for k in range(PB):
            mine = delta[k * CAP : (k + 1) * CAP]
            row = jnp.sum(jnp.where(wide, mine, 0.0), axis=0, keepdims=True)
            dl_send[b * PB + k] = jnp.broadcast_to(row, (8, HD))

    @pl.loop(0, Z)
    def _(i):
        to = lax.rem(z + i, Z)

        @pl.when(jnp.logical_not((dp == z) & (i == 0)))
        def _():
            remote(a_v.at[to], a_all.at[dp], asend, arecv, z, at(y, to)).start()

        @pl.when(i > 0)
        def _():
            remote(dl_send.at[to], dl_got.at[z], lsend, lrecv, dp, at(y, to)).start()

    @pl.when(dp == z)
    def _():
        pltpu.make_async_copy(a_v.at[z], a_all.at[dp], arecv).start()

    pltpu.make_async_copy(dl_send.at[z], dl_got.at[z], lrecv).start()

    q_t = turned(flat(qc_v[...]))
    da_t = turned(flat(dan_v[...]))
    dq_acc[...] = jnp.zeros_like(dq_acc)

    def pieces(a):
        return a.reshape(Z, CAP, HD)

    def values_grad(d):
        return pieces(jnp.transpose(dot(da_t, flat(p_v[d]))))

    def keys_grad(d):
        @pl.loop(0, NB)
        def _(b):
            some = pl.ds(b * PB, PB)
            dprobs = rows_dot(flat(da_v[some]), flat(vc_v[d]))
            ds = flat(p_v[d, some]).astype(F32) * ((dprobs - flat(delta_v[some])) * flat(c_v[some]))
            ds = ds.astype(BF16)
            ds_v[some] = blocks(ds)
            dq_acc[some] += blocks(dot(ds, flat(kc_v[d])))

        return pieces(jnp.transpose(dot(q_t, flat(ds_v[...]))))

    def part_copy(d, which):
        return remote(
            part_send.at[d - 1, which], part_got.at[d - 1, which], psend.at[d - 1, which], precv.at[d - 1, which],
            dp, at(y - d, z),
        )

    def far(d):
        part_send[d - 1, 1] = values_grad(d).astype(BF16)
        part_copy(d, 1).start()
        part_send[d - 1, 0] = keys_grad(d).astype(BF16)
        part_copy(d, 0).start()

    def weight_part():
        arrived(a_all, arecv)
        arrived(d_all.at[pl.ds(0, X)], d2recv)
        a_t = turned(flat(a_all[...]))

        @pl.loop(1, Y + 1)
        def _(i):
            to = lax.rem(y + i, Y)
            t = dot(a_t, flat(d_all[:, :, pl.ds(pl.multiple_of(to * cols_y, HD), cols_y)]))

            @pl.when(i < Y)
            def _():
                t_send[i - 1] = t.astype(BF16)
                remote(t_send.at[i - 1], t_got.at[i - 1], tsend, trecv, dp, at(to, z)).start()

            @pl.when(i == Y)
            def _():
                t_own[...] = t

    def weight_columns():
        arrived(t_got, trecv)
        t_all = t_own[...]
        for i in range(Y - 1):
            t_all = t_all + t_got[i].astype(F32)
        z_send[...] = jnp.transpose(t_all).astype(BF16).reshape(Z, cols, HD)

        @pl.loop(1, Z)
        def _(i):
            to = lax.rem(z + i, Z)
            remote(z_send.at[to], z_got.at[z], zsend, zrecv, dp, at(y, to)).start()

        pltpu.make_async_copy(z_send.at[z], z_got.at[z], zrecv).start()

    def weight_tile():
        arrived(z_got, zrecv)
        tile = z_got[0].astype(F32)
        for i in range(1, Z):
            tile = tile + z_got[i].astype(F32)
        w_all[dp] = tile

        @pl.loop(1, DP)
        def _(i):
            to = lax.rem(dp + i, DP)
            remote(w_all.at[dp], w_all.at[dp], wsend, wrecv, to, ctx).start()

    @pl.loop(0, Y - 1)
    def _(i):
        @pl.when(i < y)
        def _():
            far(y - i)

        @pl.when(i == Y - 3)
        def _():
            weight_part()

    own_dv[...] = values_grad(0)
    own_dk[...] = keys_grad(0)
    dq_send[...] = dq_acc[...].astype(BF16)

    @pl.loop(1, Z)
    def _(i):
        to = lax.rem(z + i, Z)
        remote(dq_send.at[to], dq_hbm.at[0, :, head_cols(z)], qsend, qrecv, dp, at(y, to)).start()

    pltpu.make_async_copy(dq_send.at[z], dq_hbm.at[0, :, head_cols(z)], qrecv).start()
    weight_columns()

    arrived(dl_got, lrecv)
    delta_sum = dl_got[0]
    for i in range(1, Z):
        delta_sum = delta_sum + dl_got[i]
    live_row = lax.broadcasted_iota(jnp.int32, (1, CAP), 1).astype(F32) < count
    dlogit_ref[...] = jnp.where(live_row, (1.0 - gate_row) * delta_sum[0:1, 0:CAP], 0.0)

    weight_tile()

    def add(d, _):
        for which, own in ((1, own_dv), (0, own_dk)):
            arrived(part_got.at[d - 1, which], precv.at[d - 1, which])
            own[...] += part_got[d - 1, which].astype(F32)
        return 0

    lax.fori_loop(1, Y - y, add, 0)
    dkv_send[:, 0] = own_dk[...].astype(BF16)
    dkv_send[:, 1] = own_dv[...].astype(BF16)

    @pl.loop(1, Z)
    def _(i):
        to = lax.rem(z + i, Z)
        remote(dkv_send.at[to], dkv_hbm.at[:, :, head_cols(z)], kvsend, kvrecv, dp, at(y, to)).start()

    pltpu.make_async_copy(dkv_send.at[z], dkv_hbm.at[:, :, head_cols(z)], kvrecv).start()

    arrived(w_all.at[pl.ds(0, DP - 1)], wrecv)
    for h in range(DP):
        dw_ref[:, pl.ds(h * HD, HD)] = w_all[h]

    arrived(dq_hbm, qrecv)
    most = pl.ds(0, Z - 1)
    left(own_v.at[most], send1)
    left(da_send.at[most], dasend)
    left(dl_send.at[most], lsend)
    left(dq_send.at[most], qsend)
    left(z_send.at[most], zsend)
    left(t_send, tsend)
    left(w_all.at[pl.ds(0, DP - 1)], wsend)
    left(d_all.at[pl.ds(0, 2 * X - 1)], dsend)

    @pl.when(dp != z)
    def _():
        left(a_v, asend)

    @pl.when(dp == z)
    def _():
        left(a_v.at[most], asend)

    @pl.loop(1, Y)
    def _(j):
        @pl.when(later_y(j))
        def _():
            left(far_v.at[j - 1], fsend.at[j - 1])

    @pl.loop(0, y)
    def _(j):
        left(part_send.at[j, 0], psend.at[j, 0])
        left(part_send.at[j, 1], psend.at[j, 1])

    left(dkv_send.at[most], kvsend)
    arrived(dkv_hbm, kvrecv)


def hand_out(dq_in, dkv_in, dl_in, dw_in, dq_out, dk_out, dv_out, dl_out, dw_out, sem):
    moves = (
        (dq_in, dq_out), (dkv_in.at[pl.ds(0, 1)], dk_out), (dkv_in.at[pl.ds(1, 1)], dv_out), (dl_in, dl_out), (dw_in, dw_out),
    )
    copies = [pltpu.make_async_copy(src, dst, sem.at[i]) for i, (src, dst) in enumerate(moves)]
    for copy in copies:
        copy.start()
    for copy in copies:
        copy.wait()


def solution(mesh, y_extent=4, block=8):
    dp_n, ctx_n = mesh.shape["dp"], mesh.shape["ctx"]
    z_n = ctx_n // y_extent

    def on_device(grad_out, chosen, counts, queries, keys, values, router_logit, out_weight):
        cap, width = queries.shape[1:]
        toks, model = grad_out.shape[1:]
        nq = z_n * cap
        y_n = y_extent
        cols_y = model // y_n
        cols = cols_y // z_n
        assert width == z_n * HD == dp_n * HD
        vm = pltpu.VMEM
        dma = pltpu.SemaphoreType.DMA
        scratch = [
            vm((1, cap), jnp.int32),
            vm((1, 1), jnp.int32),
            vm((1, cap), F32),
            vm((cap, width), BF16),
            vm((cap, width), BF16),
            vm((cap, width), BF16),
            vm((toks, model), BF16),
            vm((width, model), BF16),
            vm((z_n, 3 * cap + 16, HD), BF16),
            vm((z_n, 3 * cap + 16, HD), BF16),
            vm((y_n - 1, z_n, 2 * cap + 16, HD), BF16),
            vm((1, 8, nq), F32),
            vm((y_n, z_n, cap, HD), BF16),
            vm((y_n, z_n, cap, HD), BF16),
            vm((z_n, cap, HD), BF16),
            vm((z_n, cap, 1), F32),
            vm((dp_n, cap, model), BF16),
            vm((z_n, cap, HD), BF16),
            vm((z_n, cap, HD), BF16),
            vm((y_n, z_n, cap, nq), F32),
            vm((y_n, z_n, cap, nq), BF16),
            vm((z_n, cap, 1), F32),
            vm((z_n, cap, HD), BF16),
            vm((z_n, cap, HD), BF16),
            vm((z_n, 8, HD), F32),
            vm((z_n, 8, HD), F32),
            vm((z_n, cap, 1), F32),
            vm((z_n, cap, 1), F32),
            vm((z_n, cap, nq), BF16),
            vm((z_n, cap, HD), F32),
            vm((z_n, cap, HD), BF16),
            vm((y_n - 1, 2, z_n, cap, HD), BF16),
            vm((y_n - 1, 2, z_n, cap, HD), BF16),
            vm((z_n, cap, HD), F32),
            vm((z_n, cap, HD), F32),
            vm((z_n, 2, cap, HD), BF16),
            vm((dp_n, cap, HD), BF16),
            vm((y_n - 1, HD, cols_y), BF16),
            vm((y_n - 1, HD, cols_y), BF16),
            vm((HD, cols_y), F32),
            vm((z_n, cols, HD), BF16),
            vm((z_n, cols, HD), BF16),
            vm((dp_n, cols, HD), F32),
            dma((8,)),
            dma, dma((z_n,)),
            dma((y_n - 1,)), dma((y_n - 1,)),
            dma, dma,
            dma, dma((dp_n,)), dma,
            dma, dma,
            dma, dma,
            dma((y_n - 1, 2)), dma((y_n - 1, 2)),
            dma, dma,
            dma, dma,
            dma, dma,
            dma, dma,
            dma, dma,
        ]
        free = pl.BlockSpec(memory_space=pl.ANY)
        hbm = pl.BlockSpec(memory_space=pltpu.HBM)
        vmem = pl.BlockSpec(memory_space=pltpu.VMEM)
        grads = jax.ShapeDtypeStruct((1, cap, width), BF16)
        results = (
            grads,
            jax.ShapeDtypeStruct((2, cap, width), BF16),
            jax.ShapeDtypeStruct((1, cap), F32),
            jax.ShapeDtypeStruct((model // ctx_n, width), F32),
        )
        parts = pl.pallas_call(
            functools.partial(kernel, (dp_n, y_n, z_n, cap, block)),
            out_shape=results,
            in_specs=[hbm] * 8,
            out_specs=(free, free, vmem, vmem),
            scratch_shapes=scratch,
            compiler_params=pltpu.CompilerParams(
                collective_id=0, has_side_effects=True, vmem_limit_bytes=60 * 2**20
            ),
        )(grad_out, chosen, counts, queries, keys, values, router_logit, out_weight)
        dq, dk, dv, dl, dw = pl.pallas_call(
            hand_out,
            out_shape=(grads, grads, grads) + results[2:],
            in_specs=[free] * 4,
            out_specs=(hbm,) * 5,
            scratch_shapes=[dma((5,))],
        )(*parts)
        return dq, dk, dv, dl, dw.T

    return jax.shard_map(
        on_device,
        mesh=mesh,
        in_specs=(
            P("dp", "ctx", None),
            P("dp", "ctx"),
            P("dp", "ctx"),
            P("dp", "ctx", None),
            P("dp", "ctx", None),
            P("dp", "ctx", None),
            P("dp", "ctx"),
            P(),
        ),
        out_specs=(
            P("dp", "ctx", None),
            P("dp", "ctx", None),
            P("dp", "ctx", None),
            P("dp", "ctx"),
            P(None, "ctx"),
        ),
        check_vma=False,
    )
```

time: 87.3 us -> 98.1 us (1.12)
  the two profiles are of different devices: /device:TPU:81 before, /device:TPU:1 now
where the time goes in v2:
time: 98.1 us; the launch traced here: 98 us
  Pallas kernels  96.7 us (99%)
  between operations  1.29 us (1%)
    pallas_call x1, Pallas kernels, on_device(): pl.pallas_call(functools.partial(kernel, (dp_n, y_n, z_n, cap, block)), o...  72.7 us
    pallas_call x1, Pallas kernels, on_device(): pl.pallas_call(hand_out, out_shape=(grads, grads, grads) + results[2:], i...  24 us

profile of v2, /device:TPU:1, one launch (start us, length us, event | category | flops | bytes accessed | tf_op | source)
XLA Modules:
  0.0 98.0 jit_solution(8863495217746149716)
XLA Ops:
  1.3 72.7 %shard_map.119 = (bf16[1,80,1024]{2,1,0:T(8,128)(2,1)}, bf16[2,80,1024]{2,1,0:T(8,128)(2,1)}, f32[1,80]{1,0:T(1,128)}, f32[64,1024]{1,0:T(8,128)}) custom-call(bf16[1,320,2048]{2,1,0:T(8,128)(2,1)} %grad_hbm.1, s32[1,80]{1,0:T(1,128)} %chosen_hbm.1, s32[1,1]{1,0:T(1,128)S(6)} %copy.13.counts_hbm, bf16[1,80,1024]{2,1,0:T(8,128)(2,1)} %q_hbm.1, ...), custom_call_target="tpu_custom_call" | custom-call | tf_op jit(solution)/shard_map/pallas_call | solution.py:563
  74.0 24.0 %shard_map.120 = (bf16[1,80,1024]{2,1,0:T(8,128)(2,1)}, bf16[1,80,1024]{2,1,0:T(8,128)(2,1)}, bf16[1,80,1024]{2,1,0:T(8,128)(2,1)}, f32[1,80]{1,0:T(1,128)}, f32[64,1024]{1,0:T(8,128)}) custom-call(bf16[1,80,1024]{2,1,0:T(8,128)(2,1)} %get-tuple-element.14.dq_in, bf16[2,80,1024]{2,1,0:T(8,128)(2,1)} %get-tuple-element.15.dkv_in, ...), custom_call_target="tpu_custom_call" | custom-call | tf_op jit(solution)/shard_map/pallas_call | solution.py:573

commit v3 on v2

--- a/solution.py
+++ b/solution.py
@@ -11,6 +11,7 @@
 MESH = pl.DeviceIdType.MESH
 HD = 128
 CORES = 2
+HOSTS = 2
 NEG = -1e30
 F32 = jnp.float32
 BF16 = jnp.bfloat16
@@ -37,7 +38,8 @@
     d_all, da_send, da_v, s_v, p_v, m_v, a_v, dan_v, dl_send, dl_got, c_v, delta_v,
     ds_v, dq_acc, dq_send, part_send, part_got, own_dk, own_dv, dkv_send,
     a_all, t_send, t_got, t_own, z_send, z_got, w_all,
-    load_sem, send1, recv1, fsend, frecv, dasend, darecv, dsend, drecv, d2recv,
+    gq_v, gda_v, st_send, st_got, gdq_send, gdq_got, gqsend, gqrecv, gdasend, gdarecv, stsend, strecv, gdqsend, gdqrecv,
+    load_sem, send1, recv1, q1send, q1recv, fsend, frecv, dasend, darecv, dsend, drecv, d2recv,
     asend, arecv, lsend, lrecv, psend, precv, qsend, qrecv, kvsend, kvrecv,
     tsend, trecv, zsend, zrecv, wsend, wrecv,
 ):
@@ -116,7 +118,7 @@
         def _():
             greet(s, at(y, dp))
 
-    for i in range(6):
+    for i in range(5):
         load(i).wait()
     count = counts_ref[...].astype(F32)
     meta = jnp.broadcast_to(count, (16, HD)).astype(BF16)
@@ -125,7 +127,6 @@
         own_v[h, pl.ds(0, CAP), :] = k_in[:, cut]
         own_v[h, pl.ds(CAP, CAP), :] = v_in[:, cut]
         own_v[h, pl.ds(2 * CAP, 16), :] = meta
-        own_v[h, pl.ds(2 * CAP + 16, CAP), :] = q_in[:, cut]
 
     eye = lax.broadcasted_iota(jnp.int32, (CAP, CAP), 0) == lax.broadcasted_iota(jnp.int32, (CAP, CAP), 1)
 
@@ -151,6 +152,14 @@
         remote(own_v.at[to], got_v.at[z], send1, recv1.at[z], dp, at(y, to)).start()
 
     pltpu.make_async_copy(own_v.at[z], got_v.at[z], recv1.at[z]).start()
+    load(5).wait()
+
+    @pl.loop(1, Z)
+    def _(i):
+        to = lax.rem(z + offset(i), Z)
+        remote(q_in.at[:, head_cols(to)], qc_v.at[z], q1send, q1recv, dp, at(y, to)).start()
+
+    pltpu.make_async_copy(q_in.at[:, head_cols(z)], qc_v.at[z], q1recv).start()
 
     other = x * CORES + (1 - core)
     remote(d_all.at[dp], d_all.at[dp], dsend, d2recv, other, ctx).start()
@@ -189,14 +198,12 @@
         def _(j):
             @pl.when(later_y(j))
             def _():
-                kv = pl.ds(0, 2 * CAP + 16)
                 remote(
-                    got_v.at[frm, kv], far_v.at[j - 1, frm], fsend.at[j - 1], frecv.at[j - 1], dp, at(y + j, z)
+                    got_v.at[frm], far_v.at[j - 1, frm], fsend.at[j - 1], frecv.at[j - 1], dp, at(y + j, z)
                 ).start()
 
         kc_v[0, frm] = got_v[frm, pl.ds(0, CAP), :]
         vc_v[0, frm] = got_v[frm, pl.ds(CAP, CAP), :]
-        qc_v[frm] = got_v[frm, pl.ds(2 * CAP + 16, CAP), :]
         cnt = got_v[frm, pl.ds(2 * CAP, 16), :].astype(F32)[0:1, 0:1]
         rows = lax.broadcasted_iota(jnp.int32, (CAP, 1), 0).astype(F32)
         qb_v[frm] = jnp.where(rows < cnt, 0.0, NEG)
@@ -204,6 +211,16 @@
 
     kb0 = lax.fori_loop(0, Z, step, jnp.full((1, NQ), NEG, F32))
     kb_v[0] = jnp.broadcast_to(kb0, (8, NQ))
+
+    arrived(qc_v, q1recv)
+
+    def to_hosts(src, dst, ss, rs):
+        @pl.when(y == Y - 1)
+        def _():
+            for host in range(HOSTS):
+                remote(src, dst, ss.at[host], rs, dp, at(host, z)).start()
+
+    to_hosts(qc_v, gq_v, gqsend, gqrecv)
 
     def flat(a):
         return a.reshape(a.shape[0] * a.shape[1], a.shape[2])
@@ -246,13 +263,8 @@
 
     lax.fori_loop(1, y + 1, earlier, 0)
 
-    @pl.loop(1, X)
-    def _(i):
-        frm = lax.rem(x + i, X) * CORES + core
-        arrived(d_all.at[frm], drecv.at[frm])
-        remote(d_all.at[frm], d_all.at[frm], dsend, d2recv, other, ctx).start()
-
     arrived(da_v, darecv)
+    to_hosts(da_v, gda_v, gdasend, gdarecv)
 
     wide = lax.broadcasted_iota(jnp.int32, (CAP, HD), 0) == lax.broadcasted_iota(jnp.int32, (CAP, HD), 1)
 
@@ -279,11 +291,20 @@
         delta_v[some] = blocks(delta)
         c_v[some] = blocks(inv * scale)
         dan_v[some] = blocks((da * inv).astype(BF16))
+
+        @pl.when(y == Y - 1)
+        def _():
+            which = lax.broadcasted_iota(jnp.int32, (BR, HD), 1)
+            figures = jnp.where(which == 0, mc - qb, jnp.where(which == 1, delta, inv * scale))
+            st_send[...] = jnp.transpose(figures)[0:8]
+
         for k in range(PB):
             mine = delta[k * CAP : (k + 1) * CAP]
             row = jnp.sum(jnp.where(wide, mine, 0.0), axis=0, keepdims=True)
             dl_send[b * PB + k] = jnp.broadcast_to(row, (8, HD))
 
+    to_hosts(st_send, st_got, stsend, strecv)
+
     @pl.loop(0, Z)
     def _(i):
         to = lax.rem(z + i, Z)
@@ -301,6 +322,12 @@
         pltpu.make_async_copy(a_v.at[z], a_all.at[dp], arecv).start()
 
     pltpu.make_async_copy(dl_send.at[z], dl_got.at[z], lrecv).start()
+
+    @pl.loop(1, X)
+    def _(i):
+        frm = lax.rem(x + i, X) * CORES + core
+        arrived(d_all.at[frm], drecv.at[frm])
+        remote(d_all.at[frm], d_all.at[frm], dsend, d2recv, other, ctx).start()
 
     q_t = turned(flat(qc_v[...]))
     da_t = turned(flat(dan_v[...]))
@@ -381,27 +408,77 @@
             to = lax.rem(dp + i, DP)
             remote(w_all.at[dp], w_all.at[dp], wsend, wrecv, to, ctx).start()
 
-    @pl.loop(0, Y - 1)
-    def _(i):
-        @pl.when(i < y)
-        def _():
-            far(y - i)
-
-        @pl.when(i == Y - 3)
+    def queries_out():
+        dq_send[...] = dq_acc[...].astype(BF16)
+
+        @pl.loop(1, Z)
+        def _(i):
+            to = lax.rem(z + i, Z)
+            remote(dq_send.at[to], dq_hbm.at[0, :, head_cols(z)], qsend, qrecv, dp, at(y, to)).start()
+
+        pltpu.make_async_copy(dq_send.at[z], dq_hbm.at[0, :, head_cols(z)], qrecv).start()
+
+    def guest():
+        arrived(gq_v, gqrecv)
+        arrived(gda_v, gdarecv)
+        arrived(st_got, strecv)
+        figures = jnp.transpose(st_got[...])
+        top, g_delta, g_c = figures[:, 0:1], figures[:, 1:2], figures[:, 2:3]
+        s = rows_dot(flat(gq_v[...]), flat(kc_v[0])) + kb_v[0, 0:1, :]
+        p = jnp.exp2(s * c2 - top).astype(BF16)
+        p_v[Y - 1] = blocks(p)
+        g_da = flat(gda_v[...])
+        g_dan = (g_da.astype(F32) * (g_c * (1.0 / scale))).astype(BF16)
+        own_dv[...] += pieces(jnp.transpose(dot(turned(g_dan), flat(p_v[Y - 1]))))
+        dprobs = rows_dot(g_da, flat(vc_v[0]))
+        ds = (flat(p_v[Y - 1]).astype(F32) * ((dprobs - g_delta) * g_c)).astype(BF16)
+        ds_v[...] = blocks(ds)
+        gdq_send[...] = blocks(dot(ds, flat(kc_v[0]))).astype(BF16)
+        remote(gdq_send, gdq_got.at[y], gdqsend, gdqrecv.at[y], dp, at(Y - 1, z)).start()
+        own_dk[...] += pieces(jnp.transpose(dot(turned(flat(gq_v[...])), flat(ds_v[...]))))
+
+    def own():
+        own_dv[...] = values_grad(0)
+        own_dk[...] = keys_grad(0)
+
+        @pl.when(y < Y - 1)
+        def _():
+            queries_out()
+
+    n_far = y - HOSTS * (y == Y - 1).astype(jnp.int32)
+
+    @pl.loop(0, Y)
+    def _(i):
+        @pl.when(i < n_far)
+        def _():
+            far(n_far - i)
+
+        @pl.when(i == n_far)
+        def _():
+            own()
+
+        @pl.when(i == 0)
         def _():
             weight_part()
 
-    own_dv[...] = values_grad(0)
-    own_dk[...] = keys_grad(0)
-    dq_send[...] = dq_acc[...].astype(BF16)
-
-    @pl.loop(1, Z)
-    def _(i):
-        to = lax.rem(z + i, Z)
-        remote(dq_send.at[to], dq_hbm.at[0, :, head_cols(z)], qsend, qrecv, dp, at(y, to)).start()
-
-    pltpu.make_async_copy(dq_send.at[z], dq_hbm.at[0, :, head_cols(z)], qrecv).start()
-    weight_columns()
+        @pl.when((i == 2) & (y < HOSTS))
+        def _():
+            guest()
+
+        @pl.when(i == 2)
+        def _():
+            weight_columns()
+
+        @pl.when(i == 3)
+        def _():
+            weight_tile()
+
+    @pl.when(y == Y - 1)
+    def _():
+        for host in range(HOSTS):
+            arrived(gdq_got.at[host], gdqrecv.at[host])
+            dq_acc[...] += gdq_got[host].astype(F32)
+        queries_out()
 
     arrived(dl_got, lrecv)
     delta_sum = dl_got[0]
@@ -410,24 +487,24 @@
     live_row = lax.broadcasted_iota(jnp.int32, (1, CAP), 1).astype(F32) < count
     dlogit_ref[...] = jnp.where(live_row, (1.0 - gate_row) * delta_sum[0:1, 0:CAP], 0.0)
 
-    weight_tile()
-
-    def add(d, _):
-        for which, own in ((1, own_dv), (0, own_dk)):
+    for which, grad in ((1, own_dv), (0, own_dk)):
+
+        def add(d, _, which=which, grad=grad):
             arrived(part_got.at[d - 1, which], precv.at[d - 1, which])
-            own[...] += part_got[d - 1, which].astype(F32)
-        return 0
-
-    lax.fori_loop(1, Y - y, add, 0)
-    dkv_send[:, 0] = own_dk[...].astype(BF16)
-    dkv_send[:, 1] = own_dv[...].astype(BF16)
-
-    @pl.loop(1, Z)
-    def _(i):
-        to = lax.rem(z + i, Z)
-        remote(dkv_send.at[to], dkv_hbm.at[:, :, head_cols(z)], kvsend, kvrecv, dp, at(y, to)).start()
-
-    pltpu.make_async_copy(dkv_send.at[z], dkv_hbm.at[:, :, head_cols(z)], kvrecv).start()
+            grad[...] += part_got[d - 1, which].astype(F32)
+            return 0
+
+        lax.fori_loop(1, Y - y - (y < HOSTS).astype(jnp.int32), add, 0)
+        dkv_send[which] = grad[...].astype(BF16)
+
+        @pl.loop(1, Z)
+        def _(i, which=which):
+            to = lax.rem(z + i, Z)
+            remote(
+                dkv_send.at[which, to], dkv_hbm.at[which, :, head_cols(z)], kvsend.at[which], kvrecv, dp, at(y, to)
+            ).start()
+
+        pltpu.make_async_copy(dkv_send.at[which, z], dkv_hbm.at[which, :, head_cols(z)], kvrecv).start()
 
     arrived(w_all.at[pl.ds(0, DP - 1)], wrecv)
     for h in range(DP):
@@ -435,7 +512,19 @@
 
     arrived(dq_hbm, qrecv)
     most = pl.ds(0, Z - 1)
+    @pl.when(y == Y - 1)
+    def _():
+        for host in range(HOSTS):
+            left(qc_v, gqsend.at[host])
+            left(da_v, gdasend.at[host])
+            left(st_send, stsend.at[host])
+
+    @pl.when(y < HOSTS)
+    def _():
+        left(gdq_send, gdqsend)
+
     left(own_v.at[most], send1)
+    left(qc_v.at[most], q1send)
     left(da_send.at[most], dasend)
     left(dl_send.at[most], lsend)
     left(dq_send.at[most], qsend)
@@ -458,24 +547,22 @@
         def _():
             left(far_v.at[j - 1], fsend.at[j - 1])
 
-    @pl.loop(0, y)
+    @pl.loop(0, n_far)
     def _(j):
         left(part_send.at[j, 0], psend.at[j, 0])
         left(part_send.at[j, 1], psend.at[j, 1])
 
-    left(dkv_send.at[most], kvsend)
+    left(dkv_send.at[0, most], kvsend.at[0])
+    left(dkv_send.at[1, most], kvsend.at[1])
     arrived(dkv_hbm, kvrecv)
 
 
-def hand_out(dq_in, dkv_in, dl_in, dw_in, dq_out, dk_out, dv_out, dl_out, dw_out, sem):
-    moves = (
-        (dq_in, dq_out), (dkv_in.at[pl.ds(0, 1)], dk_out), (dkv_in.at[pl.ds(1, 1)], dv_out), (dl_in, dl_out), (dw_in, dw_out),
-    )
-    copies = [pltpu.make_async_copy(src, dst, sem.at[i]) for i, (src, dst) in enumerate(moves)]
-    for copy in copies:
-        copy.start()
-    for copy in copies:
-        copy.wait()
+def hand_out(dq_in, dkv_in, dl_in, dw_in, dq_out, dk_out, dv_out, dl_out, dw_out):
+    dq_out[...] = dq_in[...]
+    dk_out[...] = dkv_in[pl.ds(0, 1)]
+    dv_out[...] = dkv_in[pl.ds(1, 1)]
+    dl_out[...] = dl_in[...]
+    dw_out[...] = dw_in[...]
 
 
 def solution(mesh, y_extent=4, block=8):
@@ -501,8 +588,8 @@
             vm((cap, width), BF16),
             vm((toks, model), BF16),
             vm((width, model), BF16),
-            vm((z_n, 3 * cap + 16, HD), BF16),
-            vm((z_n, 3 * cap + 16, HD), BF16),
+            vm((z_n, 2 * cap + 16, HD), BF16),
+            vm((z_n, 2 * cap + 16, HD), BF16),
             vm((y_n - 1, z_n, 2 * cap + 16, HD), BF16),
             vm((1, 8, nq), F32),
             vm((y_n, z_n, cap, HD), BF16),
@@ -528,7 +615,7 @@
             vm((y_n - 1, 2, z_n, cap, HD), BF16),
             vm((z_n, cap, HD), F32),
             vm((z_n, cap, HD), F32),
-            vm((z_n, 2, cap, HD), BF16),
+            vm((2, z_n, cap, HD), BF16),
             vm((dp_n, cap, HD), BF16),
             vm((y_n - 1, HD, cols_y), BF16),
             vm((y_n - 1, HD, cols_y), BF16),
@@ -536,8 +623,18 @@
             vm((z_n, cols, HD), BF16),
             vm((z_n, cols, HD), BF16),
             vm((dp_n, cols, HD), F32),
+            vm((z_n, cap, HD), BF16),
+            vm((z_n, cap, HD), BF16),
+            vm((8, nq), F32),
+            vm((8, nq), F32),
+            vm((z_n, cap, HD), BF16),
+            vm((HOSTS, z_n, cap, HD), BF16),
+            dma((HOSTS,)), dma,
+            dma((HOSTS,)), dma,
+            dma((HOSTS,)), dma,
+            dma, dma((HOSTS,)),
             dma((8,)),
-            dma, dma((z_n,)),
+            dma, dma((z_n,)), dma, dma,
             dma((y_n - 1,)), dma((y_n - 1,)),
             dma, dma,
             dma, dma((dp_n,)), dma,
@@ -545,7 +642,7 @@
             dma, dma,
             dma((y_n - 1, 2)), dma((y_n - 1, 2)),
             dma, dma,
-            dma, dma,
+            dma((2,)), dma,
             dma, dma,
             dma, dma,
             dma, dma,
@@ -573,9 +670,8 @@
         dq, dk, dv, dl, dw = pl.pallas_call(
             hand_out,
             out_shape=(grads, grads, grads) + results[2:],
-            in_specs=[free] * 4,
-            out_specs=(hbm,) * 5,
-            scratch_shapes=[dma((5,))],
+            in_specs=[vmem] * 4,
+            out_specs=(vmem,) * 5,
         )(*parts)
         return dq, dk, dv, dl, dw.T
 

time: 98.1 us -> 69.9 us (0.71)
  the two profiles are of different devices: /device:TPU:1 before, /device:TPU:24 now
where the time goes in v3:
time: 69.9 us; the launch traced here: 69.8 us
  Pallas kernels  68.5 us (98%)
  between operations  1.29 us (2%)
    pallas_call x1, Pallas kernels, on_device(): pl.pallas_call(functools.partial(kernel, (dp_n, y_n, z_n, cap, block)), o...  66.5 us
    pallas_call x1, Pallas kernels, on_device(): pl.pallas_call(hand_out, out_shape=(grads, grads, grads) + results[2:], i...  2.02 us

profile of v3, /device:TPU:24, one launch (start us, length us, event | category | flops | bytes accessed | tf_op | source)
XLA Modules:
  0.0 69.8 jit_solution(7342864580307985255)
XLA Ops:
  1.3 66.5 %shard_map.119 = (bf16[1,80,1024]{2,1,0:T(8,128)(2,1)}, bf16[2,80,1024]{2,1,0:T(8,128)(2,1)}, f32[1,80]{1,0:T(1,128)}, f32[64,1024]{1,0:T(8,128)}) custom-call(bf16[1,320,2048]{2,1,0:T(8,128)(2,1)} %grad_hbm.1, s32[1,80]{1,0:T(1,128)} %chosen_hbm.1, s32[1,1]{1,0:T(1,128)S(6)} %copy.13.counts_hbm, bf16[1,80,1024]{2,1,0:T(8,128)(2,1)} %q_hbm.1, ...), custom_call_target="tpu_custom_call" | custom-call | tf_op jit(solution)/shard_map/pallas_call | solution.py:660
  67.8 2.0 %shard_map.120 = (bf16[1,80,1024]{2,1,0:T(8,128)(2,1)}, bf16[1,80,1024]{2,1,0:T(8,128)(2,1)}, bf16[1,80,1024]{2,1,0:T(8,128)(2,1)}, f32[1,80]{1,0:T(1,128)}, f32[64,1024]{1,0:T(8,128)}) custom-call(bf16[1,80,1024]{2,1,0:T(8,128)(2,1)} %get-tuple-element.14.dq_in, bf16[2,80,1024]{2,1,0:T(8,128)(2,1)} %get-tuple-element.15.dkv_in, ...), custom_call_target="tpu_custom_call" | custom-call | tf_op jit(solution)/shard_map/pallas_call | solution.py:670

commit v4 on v3

--- a/solution.py
+++ b/solution.py
@@ -118,7 +118,7 @@
         def _():
             greet(s, at(y, dp))
 
-    for i in range(5):
+    for i in (0, 3, 4):
         load(i).wait()
     count = counts_ref[...].astype(F32)
     meta = jnp.broadcast_to(count, (16, HD)).astype(BF16)
@@ -128,11 +128,30 @@
         own_v[h, pl.ds(CAP, CAP), :] = v_in[:, cut]
         own_v[h, pl.ds(2 * CAP, 16), :] = meta
 
+    pl.semaphore_wait(barrier, (Z - 1) + (Y - 1) + (DP - 1) + DP - (dp == z).astype(jnp.int32))
+
+    @pl.loop(1, Z)
+    def _(i):
+        to = lax.rem(z + offset(i), Z)
+        remote(own_v.at[to], got_v.at[z], send1, recv1.at[z], dp, at(y, to)).start()
+
+    pltpu.make_async_copy(own_v.at[z], got_v.at[z], recv1.at[z]).start()
+    load(5).wait()
+
+    @pl.loop(1, Z)
+    def _(i):
+        to = lax.rem(z + offset(i), Z)
+        remote(q_in.at[:, head_cols(to)], qc_v.at[z], q1send, q1recv, dp, at(y, to)).start()
+
+    pltpu.make_async_copy(q_in.at[:, head_cols(z)], qc_v.at[z], q1recv).start()
+
     eye = lax.broadcasted_iota(jnp.int32, (CAP, CAP), 0) == lax.broadcasted_iota(jnp.int32, (CAP, CAP), 1)
 
     def column(row):
         return jnp.sum(jnp.where(eye, row, 0.0), axis=1, keepdims=True)
 
+    load(1).wait()
+    load(2).wait()
     gate_row = jax.nn.sigmoid(logit_ref[...])
     live_col = lax.broadcasted_iota(jnp.int32, (CAP, 1), 0).astype(F32) < count
     chosen_col = column(chosen_ref[...].astype(F32))
@@ -143,23 +162,6 @@
     gate_col = column(gate_row)
     load(6).wait()
     d_all[dp] = (gate_col * dot(hot, grad_v[...])).astype(BF16)
-
-    pl.semaphore_wait(barrier, (Z - 1) + (Y - 1) + (DP - 1) + DP - (dp == z).astype(jnp.int32))
-
-    @pl.loop(1, Z)
-    def _(i):
-        to = lax.rem(z + offset(i), Z)
-        remote(own_v.at[to], got_v.at[z], send1, recv1.at[z], dp, at(y, to)).start()
-
-    pltpu.make_async_copy(own_v.at[z], got_v.at[z], recv1.at[z]).start()
-    load(5).wait()
-
-    @pl.loop(1, Z)
-    def _(i):
-        to = lax.rem(z + offset(i), Z)
-        remote(q_in.at[:, head_cols(to)], qc_v.at[z], q1send, q1recv, dp, at(y, to)).start()
-
-    pltpu.make_async_copy(q_in.at[:, head_cols(z)], qc_v.at[z], q1recv).start()
 
     other = x * CORES + (1 - core)
     remote(d_all.at[dp], d_all.at[dp], dsend, d2recv, other, ctx).start()
@@ -469,9 +471,24 @@
         def _():
             weight_columns()
 
-        @pl.when(i == 3)
-        def _():
-            weight_tile()
+    for which, grad in ((1, own_dv), (0, own_dk)):
+
+        def add(d, _, which=which, grad=grad):
+            arrived(part_got.at[d - 1, which], precv.at[d - 1, which])
+            grad[...] += part_got[d - 1, which].astype(F32)
+            return 0
+
+        lax.fori_loop(1, Y - y - (y < HOSTS).astype(jnp.int32), add, 0)
+        dkv_send[which] = grad[...].astype(BF16)
+
+        @pl.loop(1, Z)
+        def _(i, which=which):
+            to = lax.rem(z + i, Z)
+            remote(
+                dkv_send.at[which, to], dkv_hbm.at[which, :, head_cols(z)], kvsend.at[which], kvrecv, dp, at(y, to)
+            ).start()
+
+        pltpu.make_async_copy(dkv_send.at[which, z], dkv_hbm.at[which, :, head_cols(z)], kvrecv).start()
 
     @pl.when(y == Y - 1)
     def _():
@@ -480,31 +497,14 @@
             dq_acc[...] += gdq_got[host].astype(F32)
         queries_out()
 
+    weight_tile()
+
     arrived(dl_got, lrecv)
     delta_sum = dl_got[0]
     for i in range(1, Z):
         delta_sum = delta_sum + dl_got[i]
     live_row = lax.broadcasted_iota(jnp.int32, (1, CAP), 1).astype(F32) < count
     dlogit_ref[...] = jnp.where(live_row, (1.0 - gate_row) * delta_sum[0:1, 0:CAP], 0.0)
-
-    for which, grad in ((1, own_dv), (0, own_dk)):
-
-        def add(d, _, which=which, grad=grad):
-            arrived(part_got.at[d - 1, which], precv.at[d - 1, which])
-            grad[...] += part_got[d - 1, which].astype(F32)
-            return 0
-
-        lax.fori_loop(1, Y - y - (y < HOSTS).astype(jnp.int32), add, 0)
-        dkv_send[which] = grad[...].astype(BF16)
-
-        @pl.loop(1, Z)
-        def _(i, which=which):
-            to = lax.rem(z + i, Z)
-            remote(
-                dkv_send.at[which, to], dkv_hbm.at[which, :, head_cols(z)], kvsend.at[which], kvrecv, dp, at(y, to)
-            ).start()
-
-        pltpu.make_async_copy(dkv_send.at[which, z], dkv_hbm.at[which, :, head_cols(z)], kvrecv).start()
 
     arrived(w_all.at[pl.ds(0, DP - 1)], wrecv)
     for h in range(DP):

time: 69.9 us -> 67.5 us (0.966)
  the two profiles are of different devices: /device:TPU:24 before, /device:TPU:1 now
where the time goes in v4:
time: 67.5 us; the launch traced here: 66.5 us
  Pallas kernels  65.2 us (97%)
  between operations  1.29 us (2%)
    pallas_call x1, Pallas kernels, on_device(): pl.pallas_call(functools.partial(kernel, (dp_n, y_n, z_n, cap, block)), o...  63.2 us
    pallas_call x1, Pallas kernels, on_device(): pl.pallas_call(hand_out, out_shape=(grads, grads, grads) + results[2:], i...  2.02 us

profile of v4, /device:TPU:1, one launch (start us, length us, event | category | flops | bytes accessed | tf_op | source)
XLA Modules:
  0.0 66.5 jit_solution(11636613823297649939)
XLA Ops:
  1.3 63.2 %shard_map.119 = (bf16[1,80,1024]{2,1,0:T(8,128)(2,1)}, bf16[2,80,1024]{2,1,0:T(8,128)(2,1)}, f32[1,80]{1,0:T(1,128)}, f32[64,1024]{1,0:T(8,128)}) custom-call(bf16[1,320,2048]{2,1,0:T(8,128)(2,1)} %grad_hbm.1, s32[1,80]{1,0:T(1,128)} %chosen_hbm.1, s32[1,1]{1,0:T(1,128)S(6)} %copy.13.counts_hbm, bf16[1,80,1024]{2,1,0:T(8,128)(2,1)} %q_hbm.1, ...), custom_call_target="tpu_custom_call" | custom-call | tf_op jit(solution)/shard_map/pallas_call | solution.py:660
  64.4 2.0 %shard_map.120 = (bf16[1,80,1024]{2,1,0:T(8,128)(2,1)}, bf16[1,80,1024]{2,1,0:T(8,128)(2,1)}, bf16[1,80,1024]{2,1,0:T(8,128)(2,1)}, f32[1,80]{1,0:T(1,128)}, f32[64,1024]{1,0:T(8,128)}) custom-call(bf16[1,80,1024]{2,1,0:T(8,128)(2,1)} %get-tuple-element.14.dq_in, bf16[2,80,1024]{2,1,0:T(8,128)(2,1)} %get-tuple-element.15.dkv_in, ...), custom_call_target="tpu_custom_call" | custom-call | tf_op jit(solution)/shard_map/pallas_call | solution.py:670

commit v5 on v4

--- a/solution.py
+++ b/solution.py
@@ -309,7 +309,7 @@
 
     @pl.loop(0, Z)
     def _(i):
-        to = lax.rem(z + i, Z)
+        to = lax.rem(z + offset(lax.rem(Z - i, Z)), Z)
 
         @pl.when(jnp.logical_not((dp == z) & (i == 0)))
         def _():
@@ -393,7 +393,7 @@
 
         @pl.loop(1, Z)
         def _(i):
-            to = lax.rem(z + i, Z)
+            to = lax.rem(z + offset(Z - i), Z)
             remote(z_send.at[to], z_got.at[z], zsend, zrecv, dp, at(y, to)).start()
 
         pltpu.make_async_copy(z_send.at[z], z_got.at[z], zrecv).start()
@@ -415,7 +415,7 @@
 
         @pl.loop(1, Z)
         def _(i):
-            to = lax.rem(z + i, Z)
+            to = lax.rem(z + offset(Z - i), Z)
             remote(dq_send.at[to], dq_hbm.at[0, :, head_cols(z)], qsend, qrecv, dp, at(y, to)).start()
 
         pltpu.make_async_copy(dq_send.at[z], dq_hbm.at[0, :, head_cols(z)], qrecv).start()
@@ -483,7 +483,7 @@
 
         @pl.loop(1, Z)
         def _(i, which=which):
-            to = lax.rem(z + i, Z)
+            to = lax.rem(z + offset(Z - i), Z)
             remote(
                 dkv_send.at[which, to], dkv_hbm.at[which, :, head_cols(z)], kvsend.at[which], kvrecv, dp, at(y, to)
             ).start()

time: 67.5 us -> 65.7 us (0.973); the launches traced: 66.5 us -> 65.6 us
  Pallas kernels: 65.2 us -> 64.3 us
    pallas_call x1, Pallas kernels: 63.2 us -> 62.3 us  [on_device(): pl.pallas_call(functools.partial(kernel, (dp_n, y_n, z_n, cap, block)), o...]
where the time goes in v5:
time: 65.7 us; the launch traced here: 65.6 us
  Pallas kernels  64.3 us (98%)
  between operations  1.29 us (2%)
    pallas_call x1, Pallas kernels, on_device(): pl.pallas_call(functools.partial(kernel, (dp_n, y_n, z_n, cap, block)), o...  62.3 us
    pallas_call x1, Pallas kernels, on_device(): pl.pallas_call(hand_out, out_shape=(grads, grads, grads) + results[2:], i...  2.02 us

profile of v5, /device:TPU:1, one launch (start us, length us, event | category | flops | bytes accessed | tf_op | source)
XLA Modules:
  0.0 65.6 jit_solution(14523943642222621161)
XLA Ops:
  1.3 62.3 %shard_map.119 = (bf16[1,80,1024]{2,1,0:T(8,128)(2,1)}, bf16[2,80,1024]{2,1,0:T(8,128)(2,1)}, f32[1,80]{1,0:T(1,128)}, f32[64,1024]{1,0:T(8,128)}) custom-call(bf16[1,320,2048]{2,1,0:T(8,128)(2,1)} %grad_hbm.1, s32[1,80]{1,0:T(1,128)} %chosen_hbm.1, s32[1,1]{1,0:T(1,128)S(6)} %copy.13.counts_hbm, bf16[1,80,1024]{2,1,0:T(8,128)(2,1)} %q_hbm.1, ...), custom_call_target="tpu_custom_call" | custom-call | tf_op jit(solution)/shard_map/pallas_call | solution.py:660
  63.6 2.0 %shard_map.120 = (bf16[1,80,1024]{2,1,0:T(8,128)(2,1)}, bf16[1,80,1024]{2,1,0:T(8,128)(2,1)}, bf16[1,80,1024]{2,1,0:T(8,128)(2,1)}, f32[1,80]{1,0:T(1,128)}, f32[64,1024]{1,0:T(8,128)}) custom-call(bf16[1,80,1024]{2,1,0:T(8,128)(2,1)} %get-tuple-element.14.dq_in, bf16[2,80,1024]{2,1,0:T(8,128)(2,1)} %get-tuple-element.15.dkv_in, ...), custom_call_target="tpu_custom_call" | custom-call | tf_op jit(solution)/shard_map/pallas_call | solution.py:670

commit v6 on v5

--- a/solution.py
+++ b/solution.py
@@ -315,13 +315,14 @@
         def _():
             remote(a_v.at[to], a_all.at[dp], asend, arecv, z, at(y, to)).start()
 
-        @pl.when(i > 0)
-        def _():
-            remote(dl_send.at[to], dl_got.at[z], lsend, lrecv, dp, at(y, to)).start()
-
     @pl.when(dp == z)
     def _():
         pltpu.make_async_copy(a_v.at[z], a_all.at[dp], arecv).start()
+
+    @pl.loop(1, Z)
+    def _(i):
+        to = lax.rem(z + offset(Z - i), Z)
+        remote(dl_send.at[to], dl_got.at[z], lsend, lrecv, dp, at(y, to)).start()
 
     pltpu.make_async_copy(dl_send.at[z], dl_got.at[z], lrecv).start()
 

time: 65.7 us -> 66.1 us (level)
  no operation moved by 1% of the time
where the time goes in v6:
time: 66.1 us; the launch traced here: 66 us
  Pallas kernels  64.7 us (98%)
  between operations  1.29 us (2%)
    pallas_call x1, Pallas kernels, on_device(): pl.pallas_call(functools.partial(kernel, (dp_n, y_n, z_n, cap, block)), o...  62.7 us
    pallas_call x1, Pallas kernels, on_device(): pl.pallas_call(hand_out, out_shape=(grads, grads, grads) + results[2:], i...  2.02 us

profile of v6, /device:TPU:1, one launch (start us, length us, event | category | flops | bytes accessed | tf_op | source)
XLA Modules:
  0.0 66.0 jit_solution(15389043138320434345)
XLA Ops:
  1.3 62.7 %shard_map.119 = (bf16[1,80,1024]{2,1,0:T(8,128)(2,1)}, bf16[2,80,1024]{2,1,0:T(8,128)(2,1)}, f32[1,80]{1,0:T(1,128)}, f32[64,1024]{1,0:T(8,128)}) custom-call(bf16[1,320,2048]{2,1,0:T(8,128)(2,1)} %grad_hbm.1, s32[1,80]{1,0:T(1,128)} %chosen_hbm.1, s32[1,1]{1,0:T(1,128)S(6)} %copy.13.counts_hbm, bf16[1,80,1024]{2,1,0:T(8,128)(2,1)} %q_hbm.1, ...), custom_call_target="tpu_custom_call" | custom-call | tf_op jit(solution)/shard_map/pallas_call | solution.py:661
  64.0 2.0 %shard_map.120 = (bf16[1,80,1024]{2,1,0:T(8,128)(2,1)}, bf16[1,80,1024]{2,1,0:T(8,128)(2,1)}, bf16[1,80,1024]{2,1,0:T(8,128)(2,1)}, f32[1,80]{1,0:T(1,128)}, f32[64,1024]{1,0:T(8,128)}) custom-call(bf16[1,80,1024]{2,1,0:T(8,128)(2,1)} %get-tuple-element.14.dq_in, bf16[2,80,1024]{2,1,0:T(8,128)(2,1)} %get-tuple-element.15.dkv_in, ...), custom_call_target="tpu_custom_call" | custom-call | tf_op jit(solution)/shard_map/pallas_call | solution.py:671
